TPU v7x, 32 devices: a whole 2x2x4 slice. The times are simulated.
32 devices in a mesh: dp: 2 (over x), fsdp: 16 (over z, y, core).
Axes of the slice: x: 2, y: 2, z: 4, core: 2. Of those that a mesh axis runs over, the one named last changes fastest.
Arguments:
- tokens: bfloat16 [32768, 768], P(('dp', 'fsdp')), may hold values from -6 to 6
- encoded: bfloat16 [32768, 768], P(('dp', 'fsdp')), may hold values from -6 to 6
- cotangent: bfloat16 [32768, 768], P(('dp', 'fsdp')), may hold values from -6 to 6
- bucket: int32 [32], P(('dp', 'fsdp')), may hold values from 0 to 1, as said below
- target_len: int32 [32, 4], P(('dp', 'fsdp')), may hold values from 0 to 1024, as said below
- source_len: int32 [32, 4], P(('dp', 'fsdp')), may hold values from 0 to 1024, as said below
- self_in: bfloat16 [768, 2304], P('fsdp'), may hold values from -0.21875 to 0.21875
- self_bias: bfloat16 [3, 768], P(None, 'fsdp'), may hold values from -1 to 1
- self_out: bfloat16 [768, 768], P('fsdp'), may hold values from -1.25 to 1.25
- cross_q: bfloat16 [768, 768], P('fsdp'), may hold values from -0.21875 to 0.21875
- cross_kv: bfloat16 [768, 1536], P('fsdp'), may hold values from -0.21875 to 0.21875
- cross_bias: bfloat16 [3, 768], P(None, 'fsdp'), may hold values from -1 to 1
- cross_out: bfloat16 [768, 768], P('fsdp'), may hold values from -1.25 to 1.25
- ffn_in: bfloat16 [768, 3072], P('fsdp'), may hold values from -0.21875 to 0.21875
- ffn_in_bias: bfloat16 [3072], P('fsdp'), may hold values from -1 to 1
- ffn_out: bfloat16 [3072, 768], P('fsdp'), may hold values from -0.109375 to 0.109375
- ffn_out_bias: bfloat16 [768], P('fsdp'), may hold values from -1 to 1
- norm_gain: bfloat16 [3, 768], P(None, 'fsdp'), may hold values from 0.5 to 1.5
- norm_shift: bfloat16 [3, 768], P(None, 'fsdp'), may hold values from -1 to 1
Outputs:
- output: bfloat16 [32768, 768], P(('dp', 'fsdp'))
- tokens_grad: bfloat16 [32768, 768], P(('dp', 'fsdp'))
- encoded_grad: bfloat16 [32768, 768], P(('dp', 'fsdp'))
- self_in_grad: float32 [768, 2304], P('fsdp')
- self_bias_grad: float32 [3, 768], P(None, 'fsdp')
- self_out_grad: float32 [768, 768], P('fsdp')
- cross_q_grad: float32 [768, 768], P('fsdp')
- cross_kv_grad: float32 [768, 1536], P('fsdp')
- cross_bias_grad: float32 [3, 768], P(None, 'fsdp')
- cross_out_grad: float32 [768, 768], P('fsdp')
- ffn_in_grad: float32 [768, 3072], P('fsdp')
- ffn_in_bias_grad: float32 [3072], P('fsdp')
- ffn_out_grad: float32 [3072, 768], P('fsdp')
- ffn_out_bias_grad: float32 [768], P('fsdp')
- norm_gain_grad: float32 [3, 768], P(None, 'fsdp')
- norm_shift_grad: float32 [3, 768], P(None, 'fsdp')
Inputs may be any that keep to these rules, and one draw needn't show every extreme that they name: bucket[s] = 1: slot s holds one sequence of up to 1024 tokens; 0: 4 sequences of up to 256 tokens each. Both buckets occur in every draw. `target_len`: for a slot of bucket 1 the first entry is its sequence's length, 1 to 1024, and the others are 0; for bucket 0 every entry is a length of 1 to 256. Some slot's sequence has 1024 tokens and some short sequence has 256. `source_len`: laid out as target_len, for the encoder rows of each sequence; some slot's sequence has 1024 and some short sequence has 256.
All inputs are finite; a program needn't handle non-finite values.
Results may differ from a plain program's by a relative error of at most 0.024.
Values may be sent and summed in bfloat16 or wider, within the bound.
A program may use at most 448 MiB of HBM per device.

v0:
```python
from functools import partial

import jax
import jax.numpy as jnp
from jax import lax
from jax.sharding import PartitionSpec as P

D = 768
H = 12
HD = 64
LONG = 1024
SEGS = 4
SHORT = 256
BLOCK = 512


EPS = 1e-05
NEG = -1e30


def dot_plain(left_mat, right_mat):
    return jnp.dot(left_mat, right_mat, preferred_element_type=jnp.float32)


def dot_right_t(left_mat, right_mat):
    return lax.dot_general(
        left_mat, right_mat, (((1,), (1,)), ((), ())), preferred_element_type=jnp.float32
    )


def dot_left_t(left_mat, right_mat):
    return lax.dot_general(
        left_mat, right_mat, (((0,), (0,)), ((), ())), preferred_element_type=jnp.float32
    )


def layer_norm(residual, gains, shifts):
    row_mean = jnp.mean(residual, axis=-1, keepdims=True)
    centered = residual - row_mean
    variance = jnp.mean(centered * centered, axis=-1, keepdims=True)
    return centered * lax.rsqrt(variance + EPS) * gains + shifts


def column_sums(values16):
    return jnp.sum(values16.astype(jnp.float32), axis=0)


def maybe(active, compute, empty):
    if active is True:
        return compute()
    return lax.cond(active, compute, empty)


def slot_layout(kind, target_row, source_row):
    places = jnp.arange(LONG, dtype=jnp.int32)
    segment = jnp.where(kind == 1, 0, places // SHORT)
    offset = jnp.where(kind == 1, places, places % SHORT)
    picker = segment[:, None] == jnp.arange(SEGS, dtype=jnp.int32)[None, :]
    target_live = offset < jnp.sum(jnp.where(picker, target_row[None, :], 0), axis=1)
    source_live = offset < jnp.sum(jnp.where(picker, source_row[None, :], 0), axis=1)
    return (kind, places, segment, target_live, source_live)


def block_range(index):
    return slice(index * BLOCK, (index + 1) * BLOCK)


def self_plan(layout):
    kind, places, segment, target_live, source_live = layout

    def allowed(q_block, k_block):
        q_part, k_part = (block_range(q_block), block_range(k_block))
        same_segment = segment[q_part][:, None] == segment[k_part][None, :]
        causal = places[k_part][None, :] <= places[q_part][:, None]
        return same_segment & causal & target_live[k_part][None, :]

    return (allowed, [(0, 0, True), (1, 0, kind == 1), (1, 1, True)])


def cross_plan(layout):
    kind, places, segment, target_live, source_live = layout

    def allowed(q_block, k_block):
        q_part, k_part = (block_range(q_block), block_range(k_block))
        same_segment = segment[q_part][:, None] == segment[k_part][None, :]
        return same_segment & source_live[k_part][None, :]

    return (allowed, [(0, 0, True), (0, 1, kind == 1), (1, 0, kind == 1), (1, 1, True)])


def block_scores(rows, cols, allowed_block):
    scores = jnp.einsum("qhd,khd->hqk", rows, cols, preferred_element_type=jnp.float32)
    return jnp.where(allowed_block[None], scores, NEG)


def block_values(probs16, vals):
    return jnp.einsum("hqk,khd->qhd", probs16, vals, preferred_element_type=jnp.float32)


def block_dprobs(grad_rows, vals):
    return jnp.einsum("qhd,khd->hqk", grad_rows, vals, preferred_element_type=jnp.float32)


def block_grads(dscores16, probs16, rows, cols, grad_rows):
    query_part = jnp.einsum("hqk,khd->qhd", dscores16, cols, preferred_element_type=jnp.float32)
    key_part = jnp.einsum("hqk,qhd->khd", dscores16, rows, preferred_element_type=jnp.float32)
    value_part = jnp.einsum("hqk,qhd->khd", probs16, grad_rows, preferred_element_type=jnp.float32)
    return (query_part, key_part, value_part)


def empty_scores():
    return jnp.full((H, BLOCK, BLOCK), NEG, jnp.float32)


def empty_square():
    return jnp.zeros((H, BLOCK, BLOCK), jnp.float32)


def empty_rows():
    return jnp.zeros((BLOCK, H, HD), jnp.float32)


def empty_triple():
    return (empty_rows(), empty_rows(), empty_rows())


def heads_of(matrix, index):
    return matrix[block_range(index)].reshape(BLOCK, H, HD)


def attend_forward(query, keys, values, allowed, links_all):
    outputs, lse_blocks = ([], [])
    for q_block in range(LONG // BLOCK):
        rows = heads_of(query, q_block)
        links = [link for link in links_all if link[0] == q_block]
        score_list = []
        for link in links:
            cols = heads_of(keys, link[1])
            score_list.append(
                maybe(
                    link[2],
                    partial(block_scores, rows, cols, allowed(q_block, link[1])),
                    empty_scores,
                )
            )
        row_max = score_list[0].max(axis=-1)
        for scores in score_list[1:]:
            row_max = jnp.maximum(row_max, scores.max(axis=-1))
        totals = sum(
            (jnp.sum(jnp.exp(scores - row_max[..., None]), axis=-1) for scores in score_list)
        )
        lse = row_max + jnp.log(totals)
        mixed = empty_rows()
        for link, scores in zip(links, score_list):
            probs16 = jnp.exp(scores - lse[..., None]).astype(jnp.bfloat16)
            mixed = mixed + maybe(
                link[2], partial(block_values, probs16, heads_of(values, link[1])), empty_rows
            )
        outputs.append(mixed.reshape(BLOCK, D).astype(jnp.bfloat16))
        lse_blocks.append(lse)
    return (jnp.concatenate(outputs, axis=0), lse_blocks)


def attend_backward(query, keys, values, grad_att, lse_blocks, allowed, links_all):
    key_grads = [empty_rows() for index in range(LONG // BLOCK)]
    value_grads = [empty_rows() for index in range(LONG // BLOCK)]
    query_grads = []
    for q_block in range(LONG // BLOCK):
        rows = heads_of(query, q_block)
        grad_rows = heads_of(grad_att, q_block)
        lse = lse_blocks[q_block]
        links = [link for link in links_all if link[0] == q_block]
        prob_list, dprob_list = ([], [])
        for link in links:
            cols = heads_of(keys, link[1])
            scores = maybe(
                link[2], partial(block_scores, rows, cols, allowed(q_block, link[1])), empty_scores
            )
            prob_list.append(jnp.exp(scores - lse[..., None]))
            dprob_list.append(
                maybe(
                    link[2],
                    partial(block_dprobs, grad_rows, heads_of(values, link[1])),
                    empty_square,
                )
            )
        delta = sum(
            (jnp.sum(probs * dprobs, axis=-1) for probs, dprobs in zip(prob_list, dprob_list))
        )
        query_acc = empty_rows()
        for link, probs, dprobs in zip(links, prob_list, dprob_list):
            dscores16 = (probs * (dprobs - delta[..., None])).astype(jnp.bfloat16)
            probs16 = probs.astype(jnp.bfloat16)
            cols = heads_of(keys, link[1])
            terms = maybe(
                link[2],
                partial(block_grads, dscores16, probs16, rows, cols, grad_rows),
                empty_triple,
            )
            query_acc = query_acc + terms[0]
            key_grads[link[1]] = key_grads[link[1]] + terms[1]
            value_grads[link[1]] = value_grads[link[1]] + terms[2]
        query_grads.append(query_acc.reshape(BLOCK, D).astype(jnp.bfloat16))
    key_all = jnp.concatenate(key_grads, axis=0).reshape(LONG, D).astype(jnp.bfloat16)
    value_all = jnp.concatenate(value_grads, axis=0).reshape(LONG, D).astype(jnp.bfloat16)
    return (jnp.concatenate(query_grads, axis=0), key_all, value_all)


def slotted_forward(query, keys, values, layouts, plan_maker):
    outputs, lse_all = ([], [])
    for slot_id, layout in enumerate(layouts):
        rows_part = slice(slot_id * LONG, (slot_id + 1) * LONG)
        allowed, links = plan_maker(layout)
        mixed, lse_blocks = attend_forward(query, keys, values, allowed, links)
        outputs.append(mixed)
        lse_all.append(lse_blocks)
    return (outputs[0], lse_all)


def slotted_backward(query, keys, values, grad_att, lse_all, layouts, plan_maker):
    query_out, key_out, value_out = ([], [], [])
    for slot_id, layout in enumerate(layouts):
        rows_part = slice(slot_id * LONG, (slot_id + 1) * LONG)
        allowed, links = plan_maker(layout)
        grads = attend_backward(query, keys, values, grad_att, lse_all[slot_id], allowed, links)
        query_out.append(grads[0])
        key_out.append(grads[1])
        value_out.append(grads[2])
    return (query_out[0], key_out[0], value_out[0])


def body(
    tokens,
    encoded,
    cotangent,
    bucket,
    target_len,
    source_len,
    self_in,
    self_bias,
    self_out,
    cross_q,
    cross_kv,
    cross_bias,
    cross_out,
    ffn_in,
    ffn_in_bias,
    ffn_out,
    ffn_out_bias,
    norm_gain,
    norm_shift,
):
    scaling = HD ** (-0.5)
    slot_count = tokens.shape[0] // LONG
    layouts = [slot_layout(bucket[0], target_len[0], source_len[0])]
    self_w_in, self_b, self_w_out, gain_first, shift_first = (
        lax.all_gather(self_in, "fsdp", axis=0, tiled=True),
        lax.all_gather(self_bias, "fsdp", axis=1, tiled=True),
        lax.all_gather(self_out, "fsdp", axis=0, tiled=True),
        lax.all_gather(norm_gain[0], "fsdp", axis=0, tiled=True),
        lax.all_gather(norm_shift[0], "fsdp", axis=0, tiled=True),
    )
    self_b32 = self_b.astype(jnp.float32)
    mixed = dot_plain(tokens, self_w_in)
    query16 = ((mixed[:, :D] + self_b32[0]) * scaling).astype(jnp.bfloat16)
    keys16 = mixed[:, D : 2 * D].astype(jnp.bfloat16)
    values16 = (mixed[:, 2 * D :] + self_b32[1]).astype(jnp.bfloat16)
    self_att, self_lse = slotted_forward(query16, keys16, values16, layouts, self_plan)
    resid1 = tokens.astype(jnp.float32) + dot_plain(self_att, self_w_out) + self_b32[2]
    hidden1 = layer_norm(
        resid1, gain_first.astype(jnp.float32), shift_first.astype(jnp.float32)
    ).astype(jnp.bfloat16)
    cross_w_q, cross_w_kv, cross_b, cross_w_out, gain_middle, shift_middle = (
        lax.all_gather(cross_q, "fsdp", axis=0, tiled=True),
        lax.all_gather(cross_kv, "fsdp", axis=0, tiled=True),
        lax.all_gather(cross_bias, "fsdp", axis=1, tiled=True),
        lax.all_gather(cross_out, "fsdp", axis=0, tiled=True),
        lax.all_gather(norm_gain[1], "fsdp", axis=0, tiled=True),
        lax.all_gather(norm_shift[1], "fsdp", axis=0, tiled=True),
    )
    cross_b32 = cross_b.astype(jnp.float32)
    pairs = dot_plain(encoded, cross_w_kv)
    cross_query16 = ((dot_plain(hidden1, cross_w_q) + cross_b32[0]) * scaling).astype(jnp.bfloat16)
    cross_keys16 = pairs[:, :D].astype(jnp.bfloat16)
    cross_values16 = (pairs[:, D:] + cross_b32[1]).astype(jnp.bfloat16)
    cross_att, cross_lse = slotted_forward(
        cross_query16, cross_keys16, cross_values16, layouts, cross_plan
    )
    resid2 = hidden1.astype(jnp.float32) + dot_plain(cross_att, cross_w_out) + cross_b32[2]
    hidden2 = layer_norm(
        resid2, gain_middle.astype(jnp.float32), shift_middle.astype(jnp.float32)
    ).astype(jnp.bfloat16)
    ffn_w_in, ffn_b_in, ffn_w_out, ffn_b_out, gain_last, shift_last = (
        lax.all_gather(ffn_in, "fsdp", axis=0, tiled=True),
        lax.all_gather(ffn_in_bias, "fsdp", axis=0, tiled=True),
        lax.all_gather(ffn_out, "fsdp", axis=0, tiled=True),
        lax.all_gather(ffn_out_bias, "fsdp", axis=0, tiled=True),
        lax.all_gather(norm_gain[2], "fsdp", axis=0, tiled=True),
        lax.all_gather(norm_shift[2], "fsdp", axis=0, tiled=True),
    )
    pre_act = dot_plain(hidden2, ffn_w_in) + ffn_b_in.astype(jnp.float32)
    gelu_exact = partial(jax.nn.gelu, approximate=False)
    activ16 = gelu_exact(pre_act).astype(jnp.bfloat16)
    resid3 = (
        hidden2.astype(jnp.float32) + dot_plain(activ16, ffn_w_out) + ffn_b_out.astype(jnp.float32)
    )
    output = layer_norm(
        resid3, gain_last.astype(jnp.float32), shift_last.astype(jnp.float32)
    ).astype(jnp.bfloat16)
    back_w_in, back_w_out, back_gain, back_shift = (
        lax.all_gather(ffn_in, "fsdp", axis=0, tiled=True),
        lax.all_gather(ffn_out, "fsdp", axis=0, tiled=True),
        lax.all_gather(norm_gain[2], "fsdp", axis=0, tiled=True),
        lax.all_gather(norm_shift[2], "fsdp", axis=0, tiled=True),
    )
    norm_pull = jax.vjp(
        layer_norm, resid3, back_gain.astype(jnp.float32), back_shift.astype(jnp.float32)
    )[1]
    d_resid3, d_gain_last, d_shift_last = norm_pull(cotangent.astype(jnp.float32))
    d_branch3 = d_resid3.astype(jnp.bfloat16)
    d_ffn_out = dot_left_t(activ16, d_branch3)
    gelu_pull = jax.vjp(gelu_exact, pre_act)[1]
    d_pre16 = gelu_pull(dot_right_t(d_branch3, back_w_out))[0].astype(jnp.bfloat16)
    d_ffn_in = dot_left_t(hidden2, d_pre16)
    d_hidden2 = d_resid3 + dot_right_t(d_pre16, back_w_in)
    ffn_members = (
        d_ffn_in,
        column_sums(d_pre16),
        d_ffn_out,
        column_sums(d_branch3),
        d_gain_last,
        d_shift_last,
    )
    ffn_shares = (
        lax.psum_scatter(ffn_members[0], "fsdp", scatter_dimension=0, tiled=True),
        lax.psum_scatter(ffn_members[1], "fsdp", scatter_dimension=0, tiled=True),
        lax.psum_scatter(ffn_members[2], "fsdp", scatter_dimension=0, tiled=True),
        lax.psum_scatter(ffn_members[3], "fsdp", scatter_dimension=0, tiled=True),
        lax.psum_scatter(ffn_members[4], "fsdp", scatter_dimension=0, tiled=True),
        lax.psum_scatter(ffn_members[5], "fsdp", scatter_dimension=0, tiled=True),
    )
    back_q, back_kv, back_out, back_gain, back_shift = (
        lax.all_gather(cross_q, "fsdp", axis=0, tiled=True),
        lax.all_gather(cross_kv, "fsdp", axis=0, tiled=True),
        lax.all_gather(cross_out, "fsdp", axis=0, tiled=True),
        lax.all_gather(norm_gain[1], "fsdp", axis=0, tiled=True),
        lax.all_gather(norm_shift[1], "fsdp", axis=0, tiled=True),
    )
    norm_pull = jax.vjp(
        layer_norm, resid2, back_gain.astype(jnp.float32), back_shift.astype(jnp.float32)
    )[1]
    d_resid2, d_gain_middle, d_shift_middle = norm_pull(d_hidden2)
    d_branch2 = d_resid2.astype(jnp.bfloat16)
    d_cross_out = dot_left_t(cross_att, d_branch2)
    d_cross_att = dot_right_t(d_branch2, back_out).astype(jnp.bfloat16)
    dcq16, dck16, dcv16 = slotted_backward(
        cross_query16, cross_keys16, cross_values16, d_cross_att, cross_lse, layouts, cross_plan
    )
    dcq_pre = dcq16 * scaling
    d_pairs = jnp.concatenate([dck16, dcv16], axis=1)
    d_cross_q = dot_left_t(hidden1, dcq_pre)
    d_cross_kv = dot_left_t(encoded, d_pairs)
    encoded_grad = dot_right_t(d_pairs, back_kv).astype(jnp.bfloat16)
    d_hidden1 = d_resid2 + dot_right_t(dcq_pre, back_q)
    d_cross_bias = jnp.stack(
        [column_sums(dcq_pre), column_sums(dcv16), column_sums(d_branch2)], axis=0
    )
    cross_members = (
        d_cross_q,
        d_cross_kv,
        d_cross_bias,
        d_cross_out,
        d_gain_middle,
        d_shift_middle,
    )
    cross_shares = (
        lax.psum_scatter(cross_members[0], "fsdp", scatter_dimension=0, tiled=True),
        lax.psum_scatter(cross_members[1], "fsdp", scatter_dimension=0, tiled=True),
        lax.psum_scatter(cross_members[2], "fsdp", scatter_dimension=1, tiled=True),
        lax.psum_scatter(cross_members[3], "fsdp", scatter_dimension=0, tiled=True),
        lax.psum_scatter(cross_members[4], "fsdp", scatter_dimension=0, tiled=True),
        lax.psum_scatter(cross_members[5], "fsdp", scatter_dimension=0, tiled=True),
    )
    back_in, back_out, back_gain, back_shift = (
        lax.all_gather(self_in, "fsdp", axis=0, tiled=True),
        lax.all_gather(self_out, "fsdp", axis=0, tiled=True),
        lax.all_gather(norm_gain[0], "fsdp", axis=0, tiled=True),
        lax.all_gather(norm_shift[0], "fsdp", axis=0, tiled=True),
    )
    norm_pull = jax.vjp(
        layer_norm, resid1, back_gain.astype(jnp.float32), back_shift.astype(jnp.float32)
    )[1]
    d_resid1, d_gain_first, d_shift_first = norm_pull(d_hidden1)
    d_branch1 = d_resid1.astype(jnp.bfloat16)
    d_self_out = dot_left_t(self_att, d_branch1)
    d_self_att = dot_right_t(d_branch1, back_out).astype(jnp.bfloat16)
    dq16, dk16, dv16 = slotted_backward(
        query16, keys16, values16, d_self_att, self_lse, layouts, self_plan
    )
    dq_pre = dq16 * scaling
    d_mixed = jnp.concatenate([dq_pre, dk16, dv16], axis=1)
    d_self_in = dot_left_t(tokens, d_mixed)
    tokens_grad = (d_resid1 + dot_right_t(d_mixed, back_in)).astype(jnp.bfloat16)
    d_self_bias = jnp.stack(
        [column_sums(dq_pre), column_sums(dv16), column_sums(d_branch1)], axis=0
    )
    self_members = (d_self_in, d_self_bias, d_self_out, d_gain_first, d_shift_first)
    self_shares = (
        lax.psum_scatter(self_members[0], "fsdp", scatter_dimension=0, tiled=True),
        lax.psum_scatter(self_members[1], "fsdp", scatter_dimension=1, tiled=True),
        lax.psum_scatter(self_members[2], "fsdp", scatter_dimension=0, tiled=True),
        lax.psum_scatter(self_members[3], "fsdp", scatter_dimension=0, tiled=True),
        lax.psum_scatter(self_members[4], "fsdp", scatter_dimension=0, tiled=True),
    )
    self_in_share, self_bias_share, self_out_share, gain_first_share, shift_first_share = (
        self_shares
    )
    (
        cross_q_share,
        cross_kv_share,
        cross_bias_share,
        cross_out_share,
        gain_middle_share,
        shift_middle_share,
    ) = cross_shares
    (
        ffn_in_share,
        ffn_in_bias_share,
        ffn_out_share,
        ffn_out_bias_share,
        gain_last_share,
        shift_last_share,
    ) = ffn_shares
    shares = (
        self_in_share,
        self_bias_share,
        self_out_share,
        cross_q_share,
        cross_kv_share,
        cross_bias_share,
        cross_out_share,
        ffn_in_share,
        ffn_in_bias_share,
        ffn_out_share,
        ffn_out_bias_share,
        gain_first_share,
        gain_middle_share,
        gain_last_share,
        shift_first_share,
        shift_middle_share,
        shift_last_share,
    )
    halves = (
        lax.psum_scatter(
            shares[0].astype(jnp.bfloat16), "dp", scatter_dimension=0, tiled=True
        ).astype(jnp.float32),
        lax.psum_scatter(
            shares[1].astype(jnp.bfloat16), "dp", scatter_dimension=1, tiled=True
        ).astype(jnp.float32),
        lax.psum_scatter(
            shares[2].astype(jnp.bfloat16), "dp", scatter_dimension=0, tiled=True
        ).astype(jnp.float32),
        lax.psum_scatter(
            shares[3].astype(jnp.bfloat16), "dp", scatter_dimension=0, tiled=True
        ).astype(jnp.float32),
        lax.psum_scatter(
            shares[4].astype(jnp.bfloat16), "dp", scatter_dimension=0, tiled=True
        ).astype(jnp.float32),
        lax.psum_scatter(
            shares[5].astype(jnp.bfloat16), "dp", scatter_dimension=1, tiled=True
        ).astype(jnp.float32),
        lax.psum_scatter(
            shares[6].astype(jnp.bfloat16), "dp", scatter_dimension=0, tiled=True
        ).astype(jnp.float32),
        lax.psum_scatter(
            shares[7].astype(jnp.bfloat16), "dp", scatter_dimension=0, tiled=True
        ).astype(jnp.float32),
        lax.psum_scatter(
            shares[8].astype(jnp.bfloat16), "dp", scatter_dimension=0, tiled=True
        ).astype(jnp.float32),
        lax.psum_scatter(
            shares[9].astype(jnp.bfloat16), "dp", scatter_dimension=0, tiled=True
        ).astype(jnp.float32),
        lax.psum_scatter(
            shares[10].astype(jnp.bfloat16), "dp", scatter_dimension=0, tiled=True
        ).astype(jnp.float32),
        lax.psum_scatter(
            shares[11].astype(jnp.bfloat16), "dp", scatter_dimension=0, tiled=True
        ).astype(jnp.float32),
        lax.psum_scatter(
            shares[12].astype(jnp.bfloat16), "dp", scatter_dimension=0, tiled=True
        ).astype(jnp.float32),
        lax.psum_scatter(
            shares[13].astype(jnp.bfloat16), "dp", scatter_dimension=0, tiled=True
        ).astype(jnp.float32),
        lax.psum_scatter(
            shares[14].astype(jnp.bfloat16), "dp", scatter_dimension=0, tiled=True
        ).astype(jnp.float32),
        lax.psum_scatter(
            shares[15].astype(jnp.bfloat16), "dp", scatter_dimension=0, tiled=True
        ).astype(jnp.float32),
        lax.psum_scatter(
            shares[16].astype(jnp.bfloat16), "dp", scatter_dimension=0, tiled=True
        ).astype(jnp.float32),
    )
    totals = (
        lax.all_gather(halves[0].astype(jnp.bfloat16), "dp", axis=0, tiled=True).astype(
            jnp.float32
        ),
        lax.all_gather(halves[1].astype(jnp.bfloat16), "dp", axis=1, tiled=True).astype(
            jnp.float32
        ),
        lax.all_gather(halves[2].astype(jnp.bfloat16), "dp", axis=0, tiled=True).astype(
            jnp.float32
        ),
        lax.all_gather(halves[3].astype(jnp.bfloat16), "dp", axis=0, tiled=True).astype(
            jnp.float32
        ),
        lax.all_gather(halves[4].astype(jnp.bfloat16), "dp", axis=0, tiled=True).astype(
            jnp.float32
        ),
        lax.all_gather(halves[5].astype(jnp.bfloat16), "dp", axis=1, tiled=True).astype(
            jnp.float32
        ),
        lax.all_gather(halves[6].astype(jnp.bfloat16), "dp", axis=0, tiled=True).astype(
            jnp.float32
        ),
        lax.all_gather(halves[7].astype(jnp.bfloat16), "dp", axis=0, tiled=True).astype(
            jnp.float32
        ),
        lax.all_gather(halves[8].astype(jnp.bfloat16), "dp", axis=0, tiled=True).astype(
            jnp.float32
        ),
        lax.all_gather(halves[9].astype(jnp.bfloat16), "dp", axis=0, tiled=True).astype(
            jnp.float32
        ),
        lax.all_gather(halves[10].astype(jnp.bfloat16), "dp", axis=0, tiled=True).astype(
            jnp.float32
        ),
        lax.all_gather(halves[11].astype(jnp.bfloat16), "dp", axis=0, tiled=True).astype(
            jnp.float32
        ),
        lax.all_gather(halves[12].astype(jnp.bfloat16), "dp", axis=0, tiled=True).astype(
            jnp.float32
        ),
        lax.all_gather(halves[13].astype(jnp.bfloat16), "dp", axis=0, tiled=True).astype(
            jnp.float32
        ),
        lax.all_gather(halves[14].astype(jnp.bfloat16), "dp", axis=0, tiled=True).astype(
            jnp.float32
        ),
        lax.all_gather(halves[15].astype(jnp.bfloat16), "dp", axis=0, tiled=True).astype(
            jnp.float32
        ),
        lax.all_gather(halves[16].astype(jnp.bfloat16), "dp", axis=0, tiled=True).astype(
            jnp.float32
        ),
    )
    norm_gain_grad = jnp.stack([totals[11], totals[12], totals[13]], axis=0)
    norm_shift_grad = jnp.stack([totals[14], totals[15], totals[16]], axis=0)
    return (
        output,
        tokens_grad,
        encoded_grad,
        totals[0],
        totals[1],
        totals[2],
        totals[3],
        totals[4],
        totals[5],
        totals[6],
        totals[7],
        totals[8],
        totals[9],
        totals[10],
        norm_gain_grad,
        norm_shift_grad,
    )


def solution(mesh):
    return jax.shard_map(
        body,
        mesh=mesh,
        in_specs=(
            P(("dp", "fsdp"), None),
            P(("dp", "fsdp"), None),
            P(("dp", "fsdp"), None),
            P(("dp", "fsdp")),
            P(("dp", "fsdp"), None),
            P(("dp", "fsdp"), None),
            P("fsdp", None),
            P(None, "fsdp"),
            P("fsdp", None),
            P("fsdp", None),
            P("fsdp", None),
            P(None, "fsdp"),
            P("fsdp", None),
            P("fsdp", None),
            P("fsdp"),
            P("fsdp", None),
            P("fsdp"),
            P(None, "fsdp"),
            P(None, "fsdp"),
        ),
        out_specs=(
            P(("dp", "fsdp"), None),
            P(("dp", "fsdp"), None),
            P(("dp", "fsdp"), None),
            P("fsdp", None),
            P(None, "fsdp"),
            P("fsdp", None),
            P("fsdp", None),
            P("fsdp", None),
            P(None, "fsdp"),
            P("fsdp", None),
            P("fsdp", None),
            P("fsdp"),
            P("fsdp", None),
            P("fsdp"),
            P(None, "fsdp"),
            P(None, "fsdp"),
        ),
        check_vma=False,
    )
```

profile of v0, /device:TPU:0, one launch (start us, length us, event | category | flops | bytes accessed | tf_op | source)
XLA Modules:
  0.0 1448.8 jit_solution(3858239181768163744)
XLA Ops:
  13.6 23.4 %all-gather.6 = bf16[16,48,3]{1,2,0:T(4,128)(2,1)S(1)} all-gather(bf16[1,48,3]{1,2,0:T(4,128)(2,1)} %bitcast.437), channel_id=1, replica_groups=mesh['dp'=2,'fsdp'=16] {'fsdp'}, dimensions={0}, use_global_device_ids=true | all-gather | bytes 4896 | tf_op jit(solution)/shard_map/all_gather | solution.py:258
  49.7 58.4 %all-reduce.35 = (bf16[768]{0:T(1024)(128)(2,1)S(1)}, bf16[768]{0:T(1024)(128)(2,1)S(1)}, bf16[768]{0:T(1024)(128)(2,1)S(1)}, bf16[768]{0:T(1024)(128)(2,1)S(1)}...) all-reduce(bf16[768]{0:T(1024)(128)(2,1)S(1)} %dynamic-update-slice, ...), channel_id=3, replica_groups=mesh['dp'=2,'fsdp'=16] {'fsdp'}, use_global_device_ids=true, to_apply=%add.1 | all-reduce | flops 8448 | bytes 33792
  108.2 17.4 %all-gather.7 = bf16[16,48,3]{1,2,0:T(4,128)(2,1)S(1)} all-gather(bf16[1,48,3]{1,2,0:T(4,128)(2,1)S(1)} %bitcast.438), channel_id=1, replica_groups=mesh['dp'=2,'fsdp'=16] {'fsdp'}, dimensions={0}, use_global_device_ids=true | all-gather | bytes 4896 | tf_op jit(solution)/shard_map/all_gather | solution.py:276
  148.0 8.5 fusion.108
  166.3 8.0 select_reduce_fusion.2
  179.9 10.9 exponential_reduce_fusion.4
  190.8 9.3 exponential_convert_fusion.2
  225.2 9.0 fusion.32
  248.3 7.9 select_reduce_fusion.1
  261.6 10.9 exponential_reduce_fusion.2
  272.5 9.4 exponential_convert_fusion.1
  284.2 7.7 select_reduce_fusion
  297.7 11.2 exponential_reduce_fusion
  309.0 9.3 exponential_convert_fusion
  323.7 9.1 fusion.31
  338.4 8.9 fusion.30
  354.1 19.1 %conditional.21 = (f32[12,512,512]{1,2,0:T(8,128)}) conditional(s32[]{:T(128)} %convert_element_type.401, () %tuple.128, (pred[512,512]{1,0:T(8,128)(4,1)S(1)}, bf16[512,12,64]{0,2,1:T(8,128)(2,1)S(1)}, bf16[512,12,64]{0,2,1:T(8,128)(2,1)S(1)}) %tuple.396), branch_computations={%region_39.40_spmd, %region_40.41_spmd} | conditional | flops 405798912 | bytes 39583752 | solution.py:51
  360.6 12.6 copy.454
  374.3 20.6 %conditional.24 = (f32[12,512,512]{1,2,0:T(8,128)}) conditional(s32[]{:T(128)} %convert_element_type.401, () %tuple.134, (pred[512,512]{1,0:T(8,128)(4,1)}, bf16[512,12,64]{0,2,1:T(8,128)(2,1)}, bf16[512,12,64]{0,2,1:T(8,128)(2,1)}) %tuple.378), branch_computations={%region_46.47_spmd, %region_47.48_spmd} | conditional | flops 405798912 | bytes 39583752 | solution.py:51
  374.3 7.9 broadcast_select_fusion.4
  382.2 12.7 copy.456
  394.9 19.5 %conditional.27 = (f32[12,512,512]{1,2,0:T(8,128)}) conditional(s32[]{:T(128)} %convert_element_type.401, () %tuple.139, (pred[512,512]{1,0:T(8,128)(4,1)S(1)}, bf16[512,12,64]{0,2,1:T(8,128)(2,1)S(1)}, bf16[512,12,64]{0,2,1:T(8,128)(2,1)S(1)}) %tuple.395), branch_computations={%region_57.58_spmd, %region_58.59_spmd} | conditional | flops 405798912 | bytes 39583752 | solution.py:51
  401.8 12.6 copy.458
  414.4 37.7 %multiply_convert_fusion.7 = (bf16[1024,3072]{1,0:T(8,128)(2,1)}, f32[1024,3072]{1,0:T(8,128)}, f32[1024,3072]{1,0:T(8,128)}) fusion(f32[3072]{0:T(1024)S(1)} %copy-done.110, bf16[768,3072]{1,0:T(8,128)(2,1)} %all-gather.28.cloned.1.call-done, f32[1024,768]{0,1:T(8,128)} %copy-done.37, f32[768]{0:T(1024)S(1)} %copy-done.116, f32[768]{0:T(1024)S(1)} %copy-done.102, ...), kind=kOutput, calls=%fused_computation.39 | convolution fusion | flops 5043388416 | bytes 39348224 | tf_op jit(solution)/shard_map/dot_general | solution.py:22
  452.1 9.7 fusion.112
  469.3 18.9 %convert_reduce_fusion = (f32[3072]{0:T(1024)}, bf16[1024,3072]{1,0:T(8,128)(2,1)}) fusion(f32[1024,3072]{1,0:T(8,128)} %get-tuple-element.542, bf16[1024,768]{0,1:T(8,128)(2,1)} %get-tuple-element.528, bf16[3072,768]{1,0:T(8,128)(2,1)} %all-gather.30.cloned.1.call-done, f32[1024,3072]{1,0:T(8,128)} %get-tuple-element.618, f32[3072]{0:T(1024)S(1)} %copy-done.110), kind=kOutput, calls=%fused_computation.20 | convolution fusion | flops 4885312512 | bytes 37773312 | tf_op jit(solution)/shard_map/dot_general | solution.py:26
  488.3 11.6 multiply_reduce_fusion.7
  511.2 7.8 conditional.22
  511.2 7.8 fusion.114
  519.1 12.7 copy.373
  538.2 12.8 copy.380
  551.1 20.6 %multiply_reduce_fusion.5 = (f32[12,512]{1,0:T(8,128)S(1)}, f32[12,512]{1,0:T(8,128)S(1)}, f32[12,512,512]{1,2,0:T(8,128)}) fusion(f32[12,512,512]{1,2,0:T(8,128)} %copy.373, f32[12,512,512]{1,2,0:T(8,128)} %get-tuple-element.459, f32[12,512]{1,0:T(8,128)S(1)} %copy-done.76, f32[12,512,512]{1,2,0:T(8,128)} %get-tuple-element.615, ...), kind=kOutput, calls=%fused_computation.35 | convolution fusion | flops 424660992 | bytes 52240384 | tf_op jit(solution)/shard_map/qhd,khd->hqk/dot_general | solution.py:101
  571.7 25.3 %fusion.6 = (bf16[12,512,512]{1,2,0:T(8,128)(2,1)}, bf16[12,512,512]{1,2,0:T(8,128)(2,1)}, bf16[12,512,512]{1,2,0:T(8,128)(2,1)}) fusion(f32[12,512,512]{1,2,0:T(8,128)} %get-tuple-element.459, f32[12,512]{1,0:T(8,128)S(1)} %copy-done.76, f32[12,512,512]{1,2,0:T(8,128)} %copy.373, f32[12,512]{1,0:T(8,128)S(1)} %add.385, ...), kind=kLoop, calls=%fused_computation.71 | loop fusion | flops 31457280 | bytes 69517312 | tf_op jit(solution)/shard_map/convert_element_type | solution.py:193
  597.1 9.1 conditional.23
  612.2 18.6 %multiply_reduce_fusion.3 = (f32[12,512]{1,0:T(8,128)S(1)}, f32[12,512]{1,0:T(8,128)}, f32[12,512,512]{1,2,0:T(8,128)}) fusion(f32[12,512,512]{1,2,0:T(8,128)} %get-tuple-element.613, f32[12,512]{1,0:T(8,128)S(1)} %copy-done.78, pred[512,512]{0,1:T(8,128)(4,1)S(1)} %copy-done.34, f32[12,512,512]{1,2,0:T(8,128)} %copy.380, ...), kind=kOutput, calls=%fused_computation.30 | convolution fusion | flops 424660992 | bytes 52240384 | tf_op jit(solution)/shard_map/qhd,khd->hqk/dot_general | solution.py:101
  631.6 24.7 %fusion.7 = (bf16[12,512,512]{1,2,0:T(8,128)(2,1)}, bf16[12,512,512]{1,2,0:T(8,128)(2,1)}, bf16[12,512,512]{1,2,0:T(8,128)(2,1)}) fusion(f32[12,512,512]{1,2,0:T(8,128)} %get-tuple-element.460, f32[12,512]{1,0:T(8,128)S(1)} %copy-done.78, f32[12,512,512]{1,2,0:T(8,128)} %copy.380, f32[12,512]{1,0:T(8,128)S(1)} %add.387, ...), kind=kLoop, calls=%fused_computation.72 | loop fusion | flops 31457280 | bytes 69517312 | tf_op jit(solution)/shard_map/convert_element_type | solution.py:193
  656.3 9.0 conditional.26
  682.2 8.7 bitcast_add_fusion.1
  695.2 6.8 conditional.28
  702.0 12.8 copy.388
  714.8 8.3 bitcast_add_fusion
  749.1 19.8 %multiply_reduce_fusion = (f32[12,512]{1,0:T(8,128)S(1)}, f32[12,512]{1,0:T(8,128)S(1)}, f32[12,512,512]{1,2,0:T(8,128)}) fusion(f32[12,512,512]{1,2,0:T(8,128)} %get-tuple-element.605, f32[12,512]{1,0:T(8,128)S(1)} %copy-done.80, pred[512,512]{0,1:T(8,128)(4,1)S(1)} %copy-done.46, f32[12,512,512]{1,2,0:T(8,128)} %copy.388, ...), kind=kOutput, calls=%fused_computation.23 | convolution fusion | flops 424660992 | bytes 52240384 | tf_op jit(solution)/shard_map/qhd,khd->hqk/dot_general | solution.py:101
  768.9 25.5 %fusion.8 = (bf16[12,512,512]{1,2,0:T(8,128)(2,1)}, bf16[12,512,512]{1,2,0:T(8,128)(2,1)}, bf16[12,512,512]{1,2,0:T(8,128)(2,1)}) fusion(f32[12,512,512]{1,2,0:T(8,128)} %get-tuple-element.461, f32[12,512]{1,0:T(8,128)S(1)} %copy-done.80, f32[12,512,512]{1,2,0:T(8,128)} %copy.388, f32[12,512]{1,0:T(8,128)S(1)} %add.390, ...), kind=kLoop, calls=%fused_computation.73 | loop fusion | flops 31457280 | bytes 69517312 | tf_op jit(solution)/shard_map/convert_element_type | solution.py:193
  794.5 11.8 conditional.29
  806.3 7.7 convolution_bitcast_fusion.14
  814.1 8.0 bitcast_add_fusion.4
  823.5 6.9 multiply_reduce_fusion.2
  830.5 7.5 multiply_convert_fusion.2
  851.9 9.2 convolution_bitcast_fusion.12
  861.1 8.1 copy.437
  869.9 11.0 fusion.113
  885.5 9.8 fusion.117
  906.4 84.1 %reduce-scatter.51.cloned.1.call-done = f32[48,2304]{1,0:T(8,128)} async-done(((f32[768,2304]{1,0:T(8,128)}), f32[48,2304]{1,0:T(8,128)}) %reduce-scatter.51.cloned.1.call-update) | async-done | bytes 442384
  992.9 9.3 add_convert_fusion.1
  1002.3 62.4 %all-reduce.34 = (bf16[3072]{0:T(1024)(128)(2,1)S(1)}, bf16[768]{0:T(1024)(128)(2,1)S(1)}, bf16[768]{0:T(1024)(128)(2,1)S(1)}, bf16[768]{0:T(1024)(128)(2,1)S(1)...) all-reduce(f32[3072]{0:T(1024)S(1)} %copy-done.111, ...), channel_id=24, replica_groups=mesh['dp'=2,'fsdp'=16] {'fsdp'}, use_global_device_ids=true, to_apply=%region_88.89.clone | all-reduce | flops 8448 | bytes 50688
  1065.2 42.4 %reduce-scatter.43.cloned.1.call-done = f32[48,3072]{1,0:T(8,128)} async-done(((f32[768,3072]{1,0:T(8,128)}), f32[48,3072]{1,0:T(8,128)}) %reduce-scatter.43.cloned.1.call-update) | async-done | bytes 589840 | tf_op jit(solution)/shard_map/reduce_scatter | solution.py:335
  1127.5 39.4 %reduce-scatter.61.cloned.1.call-done = f32[48,3]{1,0:T(8,128)} async-done(((f32[768,3]{1,0:T(8,128)}), f32[48,3]{1,0:T(8,128)}) %reduce-scatter.61.cloned.1.call-update) | async-done | bytes 592
  1167.8 58.1 %reduce-scatter.55.cloned.1.call-done = f32[48,3]{1,0:T(8,128)} async-done(((f32[768,3]{1,0:T(8,128)}), f32[48,3]{1,0:T(8,128)}) %reduce-scatter.55.cloned.1.call-update) | async-done | bytes 592
  1231.7 108.5 %reduce-scatter.47.cloned.1.call-done = f32[192,768]{1,0:T(8,128)} async-done(((f32[3072,768]{1,0:T(8,128)}), f32[192,768]{1,0:T(8,128)}) %reduce-scatter.47.cloned.1.call-update) | async-done | bytes 589840 | tf_op jit(solution)/shard_map/reduce_scatter | solution.py:337
  1370.8 7.3 reduce-scatter.33.cloned.1.call-done
  1383.6 7.7 reduce-scatter.59.cloned.1.call-done
  1397.3 7.6 reduce-scatter.53.cloned.1.call-done
  1411.3 8.5 reduce-scatter.45.cloned.1.call-done
  1427.2 7.6 reduce-scatter.49.cloned.1.call-done
  (592 shorter events, 412.1 us)
Async XLA Ops:
  7.2 126.2 %copy-start = (bf16[1024,768]{1,0:T(8,128)(2,1)S(1)}, bf16[1024,768]{1,0:T(8,128)(2,1)}, u32[]{:S(2)}) copy-start(bf16[1024,768]{1,0:T(8,128)(2,1)} %param.50) | copy-start | bytes 4718596
  7.2 126.1 %all-gather.22.cloned.1.call-start = ((), (), s32[]{:S(2)}) async-start(), calls=%async_computation.18 | async-start | bytes 2506752 | tf_op jit(solution)/shard_map/all_gather | solution.py:275
  7.9 140.0 %all-gather.18.cloned.1.call-start = ((), (), s32[]{:S(2)}) async-start(), calls=%async_computation.16 | async-start | bytes 3760128 | tf_op jit(solution)/shard_map/all_gather | solution.py:257
  8.7 37.3 %copy-start.119 = (bf16[3,48]{1,0:T(4,128)(2,1)S(1)}, bf16[3,48]{1,0:T(4,128)(2,1)}, u32[]{:S(2)}) copy-start(bf16[3,48]{1,0:T(4,128)(2,1)} %param.66) | copy-start | bytes 868
  8.7 225.5 %all-gather.20.cloned.1.call-start = ((), (), s32[]{:S(2)}) async-start(), calls=%async_computation.17 | async-start | bytes 1253376 | tf_op jit(solution)/shard_map/all_gather | solution.py:259
  9.4 36.6 %copy-start.120 = (bf16[3,48]{1,0:T(4,128)(2,1)S(1)}, bf16[3,48]{1,0:T(4,128)(2,1)}, u32[]{:S(2)}) copy-start(bf16[3,48]{1,0:T(4,128)(2,1)} %param.67) | copy-start | bytes 868
  9.4 36.6 %copy-start.121 = (u32[32]{0:T(128)S(1)}, u32[32]{0:T(128)}, u32[]{:S(2)}) copy-start(u32[32]{0:T(128)} %constant.185) | copy-start | bytes 388
  9.4 36.6 %copy-start.122 = (u32[32]{0:T(128)S(1)}, u32[32]{0:T(128)}, u32[]{:S(2)}) copy-start(u32[32]{0:T(128)} %constant.225) | copy-start | bytes 388
  9.5 232.0 %all-gather.24.cloned.1.call-start = ((), (), s32[]{:S(2)}) async-start(), calls=%async_computation.19 | async-start | bytes 1253376 | tf_op jit(solution)/shard_map/all_gather | solution.py:274
  10.0 39.2 %copy-start.126 = (bf16[48]{0:T(256)(128)(2,1)S(1)}, bf16[48]{0:T(256)(128)(2,1)}, u32[]{:S(2)}) copy-start(bf16[48]{0:T(256)(128)(2,1)} %param.65) | copy-start | bytes 292
  10.0 39.4 %copy-start.127 = (bf16[192]{0:T(256)(128)(2,1)S(1)}, bf16[192]{0:T(256)(128)(2,1)}, u32[]{:S(2)}) copy-start(bf16[192]{0:T(256)(128)(2,1)} %param.63) | copy-start | bytes 1156
  10.1 98.1 %copy-start.123 = (bf16[3,48]{1,0:T(4,128)(2,1)S(1)}, bf16[3,48]{1,0:T(4,128)(2,1)}, u32[]{:S(2)}) copy-start(bf16[3,48]{1,0:T(4,128)(2,1)} %param.60) | copy-start | bytes 868
  10.1 337.3 %all-gather.26.cloned.1.call-start = ((), (), s32[]{:S(2)}) async-start(), calls=%async_computation.20 | async-start | bytes 1253376 | tf_op jit(solution)/shard_map/all_gather | solution.py:277
  10.7 403.8 %all-gather.28.cloned.1.call-start = ((), (), s32[]{:S(2)}) async-start(), calls=%async_computation.21 | async-start | bytes 5013504 | tf_op jit(solution)/shard_map/all_gather | solution.py:294
  11.2 440.9 %all-gather.30.cloned.1.call-start = ((), (), s32[]{:S(2)}) async-start(), calls=%async_computation.22 | async-start | bytes 5013504 | tf_op jit(solution)/shard_map/all_gather | solution.py:296
  12.0 883.5 %reduce-scatter.39.cloned.1.call-start = ((), (), s32[]{:S(2)}) async-start(), calls=%async_computation.27 | async-start | bytes 2506752 | tf_op jit(solution)/shard_map/reduce_scatter | solution.py:380
  37.1 94.1 %copy-start.66 = (bf16[1024,768]{1,0:T(8,128)(2,1)S(1)}, bf16[1024,768]{1,0:T(8,128)(2,1)}, u32[]{:S(2)}) copy-start(bf16[1024,768]{1,0:T(8,128)(2,1)} %param.51) | copy-start | bytes 4718596
  108.1 130.4 %copy-start.88 = (f32[768]{0:T(1024)}, f32[768]{0:T(1024)S(1)}, u32[]{:S(2)}) copy-start(f32[768]{0:T(1024)S(1)} %convert_element_type.511) | copy-start | bytes 9220
  128.1 210.3 %copy-start.33 = (pred[512,512]{0,1:T(8,128)(4,1)}, pred[512,512]{0,1:T(8,128)(4,1)S(1)}, u32[]{:S(2)}) copy-start(pred[512,512]{0,1:T(8,128)(4,1)S(1)} %copy.366) | copy-start | bytes 786436
  141.0 213.0 %copy-start.10 = (bf16[512,768]{0,1:T(8,128)(2,1)}, bf16[512,768]{0,1:T(8,128)(2,1)S(1)}, u32[]{:S(2)}) copy-start(bf16[512,768]{0,1:T(8,128)(2,1)S(1)} %copy.359) | copy-start | bytes 2359300
  163.7 231.2 %copy-start.8 = (bf16[512,768]{0,1:T(8,128)(2,1)}, bf16[512,768]{0,1:T(8,128)(2,1)S(1)}, u32[]{:S(2)}) copy-start(bf16[512,768]{0,1:T(8,128)(2,1)S(1)} %copy.344) | copy-start | bytes 2359300
  190.8 34.4 %copy-start.79 = (f32[12,512]{1,0:T(8,128)}, f32[12,512]{1,0:T(8,128)S(1)}, u32[]{:S(2)}) copy-start(f32[12,512]{1,0:T(8,128)S(1)} %fusion.50) | copy-start | bytes 73732
  272.5 51.2 %copy-start.75 = (f32[12,512]{1,0:T(8,128)}, f32[12,512]{1,0:T(8,128)S(1)}, u32[]{:S(2)}) copy-start(f32[12,512]{1,0:T(8,128)S(1)} %fusion.49) | copy-start | bytes 73732
  309.0 29.4 %copy-start.77 = (f32[12,512]{1,0:T(8,128)}, f32[12,512]{1,0:T(8,128)S(1)}, u32[]{:S(2)}) copy-start(f32[12,512]{1,0:T(8,128)S(1)} %fusion.48) | copy-start | bytes 73732
  351.3 148.6 %copy-start.90 = (f32[1024]{0:T(1024)}, f32[1024]{0:T(1024)S(1)}, u32[]{:S(2)}) copy-start(f32[1024]{0:T(1024)S(1)} %broadcast_multiply_fusion.1) | copy-start | bytes 12292
  354.0 145.9 %copy-start.104 = (f32[1024]{0:T(1024)}, f32[1024]{0:T(1024)S(1)}, u32[]{:S(2)}) copy-start(f32[1024]{0:T(1024)S(1)} %fusion.66) | copy-start | bytes 12292
  394.9 19.5 %copy-start.102 = (f32[768]{0:T(1024)S(1)}, f32[768]{0:T(1024)}, u32[]{:S(2)}) copy-start(f32[768]{0:T(1024)} %convert_element_type.513) | copy-start | bytes 9220
  394.9 19.5 %copy-start.110 = (f32[3072]{0:T(1024)S(1)}, f32[3072]{0:T(1024)}, u32[]{:S(2)}) copy-start(f32[3072]{0:T(1024)} %convert_element_type.425) | copy-start | bytes 36868
  394.9 19.5 %copy-start.116 = (f32[768]{0:T(1024)S(1)}, f32[768]{0:T(1024)}, u32[]{:S(2)}) copy-start(f32[768]{0:T(1024)} %convert_element_type.514) | copy-start | bytes 9220
  414.4 37.7 %copy-start.118 = (f32[768]{0:T(1024)S(1)}, f32[768]{0:T(1024)}, u32[]{:S(2)}) copy-start(f32[768]{0:T(1024)} %convert_element_type.427) | copy-start | bytes 9220
  511.2 20.6 %copy-start.25 = (bf16[512,768]{0,1:T(8,128)(2,1)}, bf16[512,768]{0,1:T(8,128)(2,1)S(1)}, u32[]{:S(2)}) copy-start(bf16[512,768]{0,1:T(8,128)(2,1)S(1)} %get-tuple-element.565) | copy-start | bytes 2359300
  519.0 12.7 copy-start.23
  538.2 12.9 copy-start.28
  538.2 12.9 copy-start.35
  538.2 12.9 copy-start.76
  551.0 346.1 %reduce-scatter.35.cloned.1.call-start = ((), (), s32[]{:S(2)}) async-start(), calls=%async_computation.25 | async-start | bytes 2506752 | tf_op jit(solution)/shard_map/reduce_scatter | solution.py:377
  571.7 25.4 %copy-start.11 = (bf16[512,768]{0,1:T(8,128)(2,1)S(1)}, bf16[512,768]{0,1:T(8,128)(2,1)}, u32[]{:S(2)}) copy-start(bf16[512,768]{0,1:T(8,128)(2,1)} %copy-done.10) | copy-start | bytes 2359300
  571.7 25.4 %copy-start.14 = (bf16[512,768]{0,1:T(8,128)(2,1)S(1)}, bf16[512,768]{0,1:T(8,128)(2,1)}, u32[]{:S(2)}) copy-start(bf16[512,768]{0,1:T(8,128)(2,1)} %copy.357) | copy-start | bytes 2359300
  571.7 25.4 %copy-start.29 = (bf16[512,768]{0,1:T(8,128)(2,1)S(1)}, bf16[512,768]{0,1:T(8,128)(2,1)}, u32[]{:S(2)}) copy-start(bf16[512,768]{0,1:T(8,128)(2,1)} %get-tuple-element.564) | copy-start | bytes 2359300
  631.6 24.7 %copy-start.16 = (bf16[512,768]{0,1:T(8,128)(2,1)S(1)}, bf16[512,768]{0,1:T(8,128)(2,1)}, u32[]{:S(2)}) copy-start(bf16[512,768]{0,1:T(8,128)(2,1)} %copy.364) | copy-start | bytes 2359300
  631.6 24.7 %copy-start.26 = (bf16[512,768]{0,1:T(8,128)(2,1)S(1)}, bf16[512,768]{0,1:T(8,128)(2,1)}, u32[]{:S(2)}) copy-start(bf16[512,768]{0,1:T(8,128)(2,1)} %copy-done.25) | copy-start | bytes 2359300
  690.9 207.9 %reduce-scatter.31.cloned.1.call-start = ((), (), s32[]{:S(2)}) async-start(), calls=%async_computation.23 | async-start | bytes 2506752 | tf_op jit(solution)/shard_map/reduce_scatter | solution.py:411
  695.2 53.9 %copy-start.42 = (bf16[512,768]{0,1:T(8,128)(2,1)}, bf16[512,768]{0,1:T(8,128)(2,1)S(1)}, u32[]{:S(2)}) copy-start(bf16[512,768]{0,1:T(8,128)(2,1)S(1)} %get-tuple-element.563) | copy-start | bytes 2359300
  702.0 12.8 copy-start.27
  748.8 151.6 %reduce-scatter.57.cloned.1.call-start = ((), (), s32[]{:S(2)}) async-start(), calls=%async_computation.36 | async-start | bytes 5013504
  768.9 25.6 %copy-start.9 = (bf16[512,768]{0,1:T(8,128)(2,1)S(1)}, bf16[512,768]{0,1:T(8,128)(2,1)}, u32[]{:S(2)}) copy-start(bf16[512,768]{0,1:T(8,128)(2,1)} %copy-done.8) | copy-start | bytes 2359300
  768.9 25.6 %copy-start.19 = (bf16[512,768]{0,1:T(8,128)(2,1)S(1)}, bf16[512,768]{0,1:T(8,128)(2,1)}, u32[]{:S(2)}) copy-start(bf16[512,768]{0,1:T(8,128)(2,1)} %copy.346) | copy-start | bytes 2359300
  768.9 25.6 %copy-start.43 = (bf16[512,768]{0,1:T(8,128)(2,1)S(1)}, bf16[512,768]{0,1:T(8,128)(2,1)}, u32[]{:S(2)}) copy-start(bf16[512,768]{0,1:T(8,128)(2,1)} %copy-done.42) | copy-start | bytes 2359300
  806.2 184.2 %reduce-scatter.51.cloned.1.call-start = ((), (), s32[]{:S(2)}) async-start(), calls=%async_computation.33 | async-start | bytes 7520256
  806.3 17.2 %slice-start = ((s8[12582912]{0:T(1024)(128)(4,1)}), s8[4194304]{0:T(1024)(128)(4,1)S(1)}, s32[]{:S(2)}) async-start(s8[12582912]{0:T(1024)(128)(4,1)} %bitcast.328), calls=%async_computation.39 | async-start | bytes 8388608
  806.3 17.2 %slice-start.1 = ((s8[12582912]{0:T(1024)(128)(4,1)}), s8[4194304]{0:T(1024)(128)(4,1)S(1)}, s32[]{:S(2)}) async-start(s8[12582912]{0:T(1024)(128)(4,1)} %bitcast.328), calls=%async_computation.40 | async-start | bytes 8388608
  869.2 238.3 %reduce-scatter.43.cloned.1.call-start = ((), (), s32[]{:S(2)}) async-start(), calls=%async_computation.29 | async-start | bytes 10027008 | tf_op jit(solution)/shard_map/reduce_scatter | solution.py:335
  880.9 286.0 %reduce-scatter.61.cloned.1.call-start = ((), (), s32[]{:S(2)}) async-start(), calls=%async_computation.38 | async-start | bytes 417792
  884.4 341.4 %reduce-scatter.55.cloned.1.call-start = ((), (), s32[]{:S(2)}) async-start(), calls=%async_computation.35 | async-start | bytes 417792
  885.5 454.7 %reduce-scatter.47.cloned.1.call-start = ((), (), s32[]{:S(2)}) async-start(), calls=%async_computation.31 | async-start | bytes 10027008 | tf_op jit(solution)/shard_map/reduce_scatter | solution.py:337
  895.4 97.5 %copy-start.107 = (f32[1024]{0:T(1024)S(1)}, f32[1024]{0:T(1024)}, u32[]{:S(2)}) copy-start(f32[1024]{0:T(1024)} %copy-done.106) | copy-start | bytes 12292
  895.4 458.9 %reduce-scatter.41.cloned.1.call-start = ((), (), s32[]{:S(2)}) async-start(), calls=%async_computation.28 | async-start | bytes 110592 | tf_op jit(solution)/shard_map/reduce_scatter | solution.py:472
  897.0 468.3 %reduce-scatter.37.cloned.1.call-start = ((), (), s32[]{:S(2)}) async-start(), calls=%async_computation.26 | async-start | bytes 110592 | tf_op jit(solution)/shard_map/reduce_scatter | solution.py:463
  898.7 479.4 %reduce-scatter.33.cloned.1.call-start = ((), (), s32[]{:S(2)}) async-start(), calls=%async_computation.24 | async-start | bytes 110592 | tf_op jit(solution)/shard_map/reduce_scatter | solution.py:460
  900.4 491.0 %reduce-scatter.59.cloned.1.call-start = ((), (), s32[]{:S(2)}) async-start(), calls=%async_computation.37 | async-start | bytes 221184 | tf_op jit(solution)/shard_map/reduce_scatter | solution.py:466
  902.5 502.4 %reduce-scatter.53.cloned.1.call-start = ((), (), s32[]{:S(2)}) async-start(), calls=%async_computation.34 | async-start | bytes 331776 | tf_op jit(solution)/shard_map/reduce_scatter | solution.py:454
  992.8 427.0 %reduce-scatter.45.cloned.1.call-start = ((), (), s32[]{:S(2)}) async-start(), calls=%async_computation.30 | async-start | bytes 442368 | tf_op jit(solution)/shard_map/reduce_scatter | solution.py:475
  1002.2 115.5 %copy-start.58 = (bf16[1024,768]{0,1:T(8,128)(2,1)S(1)}, bf16[1024,768]{0,1:T(8,128)(2,1)}, u32[]{:S(2)}) copy-start(bf16[1024,768]{0,1:T(8,128)(2,1)} %get-tuple-element.559) | copy-start | bytes 4718596
  1109.4 325.4 %reduce-scatter.49.cloned.1.call-start = ((), (), s32[]{:S(2)}) async-start(), calls=%async_computation.32 | async-start | bytes 442368 | tf_op jit(solution)/shard_map/reduce_scatter | solution.py:481
  (100 other events, 532.6 us)
Sparse Core Ops, SparseCore 0:
  10.3 44.8 all-gather.21
  57.5 46.1 all-gather.17
  106.0 37.3 all-gather.19
  145.5 37.2 all-gather.23
  185.0 37.3 all-gather.25
  224.5 52.3 all-gather.27
  279.1 51.9 all-gather.29
  551.1 61.7 reduce-scatter.38
  691.0 61.8 reduce-scatter.34
  756.5 61.9 reduce-scatter.30
  822.9 74.5 reduce-scatter.56
  901.3 89.1 reduce-scatter.50
  995.1 112.3 reduce-scatter.42
  1111.5 55.4 reduce-scatter.60
  1171.3 54.5 reduce-scatter.54
  1229.8 110.3 reduce-scatter.46
  1342.9 9.6 reduce-scatter.40
  1355.3 9.9 reduce-scatter.36
  1368.2 9.8 reduce-scatter.32
  1380.8 10.4 reduce-scatter.58
  1393.6 11.1 reduce-scatter.52
  1407.8 12.0 reduce-scatter.44
  1422.7 12.0 reduce-scatter.48
where the time goes:
time: 1460 us; the launch traced here: 1450 us
  matrix products  457 us (31%)
  waiting for transfers between devices  381 us (26%)
  blocking collectives  218 us (15%)
  other arithmetic  193 us (13%)
  local copies, waits for them, and re-layouts  173 us (12%)
  between operations  22 us (2%)
    unnamed x27, waiting for transfers between devices  186 us
    unnamed x4, blocking collectives  131 us
    reduce_scatter x1, waiting for transfers between devices, body(): lax.psum_scatter(ffn_members[2], 'fsdp', scatter_dimension=0, tiled=True)  109 us
    dot_general x7, matrix products, block_dprobs(): jnp.einsum('qhd,khd->hqk', grad_rows, vals, preferred_element_type=jnp.fl...  86.5 us
    cond x6, local copies, waits for them, and re-layouts, maybe(): return lax.cond(active, compute, empty)  76.2 us
    convert_element_type x3, other arithmetic, attend_backward(): probs16 = probs.astype(jnp.bfloat16)  75.5 us
    dot_general x7, matrix products, dot_plain(): return jnp.dot(left_mat, right_mat, preferred_element_type=jnp.float32)  73 us
    dot_general x10, matrix products, block_scores(): jnp.einsum('qhd,khd->hqk', rows, cols, preferred_element_type=jnp.float32)  57.2 us
  transfers between devices with their start and end apart: 23, of which 11 were waited for; matrix products, arithmetic and copies ran while one was open for 49% of the time, Pallas kernels for 0%

commit v1 on v0

v1 whole, which is shorter than its diff:
```python
from functools import partial

import jax
import jax.numpy as jnp
from jax import lax
from jax.experimental import pallas as pl
from jax.experimental.pallas import tpu as pltpu
from jax.sharding import PartitionSpec as P

D = 768
H = 12
HD = 64
FF = 3072
LONG = 1024
SEGS = 4
SHORT = 256
PAIRS = H // 2
WIDE = 2 * HD

EPS = 1e-05
NEG = -1e30
SCALE = HD ** (-0.5)
F32 = jnp.float32
BF16 = jnp.bfloat16
MESH_ID = pl.DeviceIdType.MESH
VMEM_LIMIT = 56 << 20

SELF_B, CROSS_B, GAIN, SHIFT, OUT_B, IN_B = 0, 3, 6, 9, 12, 13
VEC_ROWS = 17
PACK = 2048


def mm(left, right, left_dim=1, right_dim=0):
    return lax.dot_general(
        left, right, (((left_dim,), (right_dim,)), ((), ())), preferred_element_type=F32
    )


def params(**kwargs):
    return pltpu.CompilerParams(vmem_limit_bytes=VMEM_LIMIT, **kwargs)


def cost(flops, nbytes, trans=0):
    return pl.CostEstimate(flops=int(flops), bytes_accessed=int(nbytes), transcendentals=int(trans))


def any_spec():
    return pl.BlockSpec(memory_space=pl.ANY)


def whole(shape):
    return pl.BlockSpec(shape, lambda *_: (0,) * len(shape))


def normed(resid):
    centered = resid - jnp.mean(resid, axis=-1, keepdims=True)
    inv = lax.rsqrt(jnp.mean(centered * centered, axis=-1, keepdims=True) + EPS)
    return centered * inv, inv


def norm_back(xhat, inv, gain, grad):
    scaled = grad * gain
    first = jnp.mean(scaled, axis=-1, keepdims=True)
    second = jnp.mean(scaled * xhat, axis=-1, keepdims=True)
    return (scaled - first - xhat * second) * inv


def col_sum(values):
    return jnp.sum(values, axis=0, keepdims=True)


def my_place():
    dp, index = lax.axis_index("dp"), lax.axis_index("fsdp")
    return dp, index // 4, (index // 2) % 2, index % 2


def place(dp, z, y, core):
    return {"dp": dp, "fsdp": (z * 2 + y) * 2 + core}


def neighbours():
    x, z, y, c = my_place()
    return [place(x, (z + k) % 4, y, c) for k in (1, 2, 3)] + [
        place(1 - x, z, y, c),
        place(x, z, 1 - y, c),
        place(x, z, y, 1 - c),
    ]


def greet():
    barrier = pltpu.get_barrier_semaphore()
    others = neighbours()
    for other in others:
        pl.semaphore_signal(barrier, inc=1, device_id=other, device_id_type=MESH_ID)
    pl.semaphore_wait(barrier, len(others))


def remote(src, dst, sems, index, device):
    return pltpu.make_async_remote_copy(
        src_ref=src,
        dst_ref=dst,
        send_sem=sems.at[0, index],
        recv_sem=sems.at[1, index],
        device_id=device,
        device_id_type=MESH_ID,
    )


GATHER_COPIES = 11


def gather_copies(shard, full, sems, local_sem):
    x, z, y, c = my_place()
    half = shard.shape[1] // 2
    mine = pl.ds(pl.multiple_of(x * half, 128), half)
    other = pl.ds(pl.multiple_of((1 - x) * half, 128), half)
    to_x, to_y, to_c = place(1 - x, z, y, c), place(x, z, 1 - y, c), place(x, z, y, 1 - c)

    def same(index, where, device):
        ref = full.at[where]
        return remote(ref, ref, sems, index, device)

    own = (slice(None), y, c, slice(None), mine)
    from_x = (slice(None), y, c, slice(None), other)
    from_y = (slice(None), 1 - y, c, slice(None), mine)
    diagonal = (slice(None), 1 - y, c, slice(None), other)
    copies = [
        remote(shard.at[:, mine], full.at[z, y, c, :, mine], sems, k - 1, place(x, (z + k) % 4, y, c))
        for k in (1, 2, 3)
    ]
    copies += [same(3, own, to_x), same(4, own, to_y)]
    copies += [
        same(5, (pl.ds(0, 2), 1 - y, c, slice(None), mine), to_x),
        same(6, (pl.ds(2, 2), y, c, slice(None), other), to_y),
    ]
    copies += [same(7, own, to_c), same(8, from_x, to_c), same(9, from_y, to_c), same(10, diagonal, to_c)]
    local = pltpu.make_async_copy(shard.at[:, mine], full.at[z, y, c, :, mine], local_sem)
    return copies, local


def gather_steps(shard, full, sems, local_sem):
    copies, local = gather_copies(shard, full, sems, local_sem)

    def first():
        local.start()
        for copy in copies[:3]:
            copy.start()

    def second():
        local.wait()
        for copy in copies[:3]:
            copy.wait_recv()
        for index in (3, 4, 7):
            copies[index].start()

    def third():
        copies[3].wait_recv()
        copies[4].wait_recv()
        for index in (5, 6, 8, 9):
            copies[index].start()

    def fourth():
        copies[5].wait_recv()
        copies[6].wait_recv()
        copies[10].start()

    def last():
        for index in (7, 8, 9, 10):
            copies[index].wait_recv()
        for copy in copies:
            copy.wait_send()

    return [first, second, third, fourth, last]


SMALL_COPIES = 5


def small_gather_steps(shard, full, sems, local_sem):
    x, z, y, c = my_place()
    local = pltpu.make_async_copy(shard, full.at[z, y, c], local_sem)
    copies = [
        remote(shard, full.at[z, y, c], sems, k - 1, place(x, (z + k) % 4, y, c)) for k in (1, 2, 3)
    ]
    copies.append(remote(full.at[:, y, c], full.at[:, y, c], sems, 3, place(x, z, 1 - y, c)))
    copies.append(remote(full.at[:, :, c], full.at[:, :, c], sems, 4, place(x, z, y, 1 - c)))

    def first():
        local.start()
        for copy in copies[:3]:
            copy.start()

    def second():
        local.wait()
        for copy in copies[:3]:
            copy.wait_recv()
        copies[3].start()

    def third():
        copies[3].wait_recv()
        copies[4].start()

    def last():
        copies[4].wait_recv()
        for copy in copies:
            copy.wait_send()

    return [first, second, third, last]


def gather_kernel(count, small, *refs):
    total = count + small
    shards, fulls = refs[:total], refs[total : 2 * total]
    sems = refs[2 * total :]
    greet()
    plans = [
        gather_steps(shards[i], fulls[i], sems[2 * i], sems[2 * i + 1].at[0]) for i in range(count)
    ]
    if small:
        plans.append(
            small_gather_steps(shards[count], fulls[count], sems[2 * count], sems[2 * count + 1].at[0])
        )
    for step in range(5):
        for plan in plans:
            if step < len(plan):
                plan[step]()


def gather_scratch(count, small):
    scratch = []
    for _ in range(count):
        scratch += [pltpu.SemaphoreType.DMA((2, GATHER_COPIES)), pltpu.SemaphoreType.DMA((1,))]
    if small:
        scratch += [pltpu.SemaphoreType.DMA((2, SMALL_COPIES)), pltpu.SemaphoreType.DMA((1,))]
    return scratch


def gather_shape(shard):
    return jax.ShapeDtypeStruct((4, 2, 2) + shard.shape, shard.dtype)


def gather_call(shards, small, collective_id, name):
    count = len(shards)
    arrays = list(shards) + ([small] if small is not None else [])
    has_small = int(small is not None)
    return pl.pallas_call(
        partial(gather_kernel, count, has_small),
        out_shape=[gather_shape(a) for a in arrays],
        in_specs=[any_spec()] * len(arrays),
        out_specs=[any_spec()] * len(arrays),
        scratch_shapes=gather_scratch(count, has_small),
        compiler_params=params(collective_id=collective_id, has_side_effects=True),
        name=name,
    )(*arrays)


SCATTER_COPIES = 10


def scatter_scratch(rows, cols):
    half = cols // 2
    return [
        pltpu.VMEM((4, 2, 2, rows, half), BF16),
        pltpu.VMEM((4, 2, 2, rows, half), BF16),
        pltpu.VMEM((2, 2, rows, half), BF16),
        pltpu.VMEM((2, rows, half), BF16),
        pltpu.VMEM((2, 2, rows, half), BF16),
        pltpu.VMEM((2, rows, half), BF16),
        pltpu.VMEM((4, rows, half), BF16),
        pltpu.VMEM((3, rows, half), BF16),
        pltpu.VMEM((rows, half), BF16),
        pltpu.VMEM((rows, half), BF16),
        pltpu.SemaphoreType.DMA((2, SCATTER_COPIES)),
        pltpu.SemaphoreType.DMA((2,)),
    ]


SCATTER_REFS = 12


def add_into(dst, left, right):
    dst[...] = (left[...].astype(F32) + right[...].astype(F32)).astype(BF16)


def scatter_steps(grads, share, bufs):
    own, peer, x_one, x_two, y_one, y_two, quarter, z_in, half_mine, half_other, sems, local = bufs
    x, z, y, c = my_place()
    half = own.shape[-1]
    to_x, to_y, to_c = place(1 - x, z, y, c), place(x, z, 1 - y, c), place(x, z, y, 1 - c)
    cols = [pl.ds(h * half, half) for h in range(2)]
    loads = [
        pltpu.make_async_copy(grads.at[:, :, c, :, cols[h]], own.at[:, :, h], local.at[h])
        for h in range(2)
    ]
    swaps = [
        remote(grads.at[:, :, 1 - c, :, cols[h]], peer.at[:, :, h], sems, h, to_c) for h in range(2)
    ]
    x_first = remote(own.at[pl.ds(0, 2), :, 1 - x], x_one, sems, 2, to_x)
    y_first = remote(own.at[pl.ds(2, 2), 1 - y], y_one, sems, 3, to_y)
    x_second = remote(own.at[pl.ds(2, 2), y, 1 - x], x_two, sems, 4, to_x)
    y_second = remote(own.at[pl.ds(0, 2), 1 - y, x], y_two, sems, 5, to_y)
    z_sends = [
        remote(quarter.at[(z + k) % 4], z_in.at[k - 1], sems, 5 + k, place(x, (z + k) % 4, y, c))
        for k in (1, 2, 3)
    ]
    last_swap = remote(half_mine, half_other, sems, 9, to_x)

    def start():
        for copy in loads + swaps:
            copy.start()

    def sum_cores():
        for copy in loads:
            copy.wait()
        for copy in swaps:
            copy.wait_recv()

        @pl.loop(0, 16)
        def _(i):
            place_of = (i // 4, (i // 2) % 2, i % 2)
            add_into(own.at[place_of], own.at[place_of], peer.at[place_of])

        x_first.start()
        y_first.start()

    def sum_first():
        x_first.wait_recv()
        y_first.wait_recv()

        @pl.loop(0, 2)
        def _(i):
            add_into(own.at[i, 1 - y, x], own.at[i, 1 - y, x], x_one.at[i, 1 - y])
            add_into(own.at[2 + i, y, 1 - x], own.at[2 + i, y, 1 - x], y_one.at[i, 1 - x])

        x_second.start()
        y_second.start()

        @pl.loop(0, 2)
        def _(i):
            add_into(own.at[i, y, x], own.at[i, y, x], x_one.at[i, y])
            add_into(own.at[2 + i, y, x], own.at[2 + i, y, x], y_one.at[i, x])

    def sum_second():
        x_second.wait_recv()
        y_second.wait_recv()

        @pl.loop(0, 2)
        def _(i):
            add_into(quarter.at[i], own.at[i, y, x], y_two.at[i])
            add_into(quarter.at[2 + i], own.at[2 + i, y, x], x_two.at[i])

        for copy in z_sends:
            copy.start()

    def sum_z():
        for copy in z_sends:
            copy.wait_recv()
        total = quarter[z].astype(F32)
        for k in range(3):
            total = total + z_in[k].astype(F32)
        half_mine[...] = total.astype(BF16)
        last_swap.start()

    def finish():
        last_swap.wait_recv()
        share[:, pl.ds(pl.multiple_of(x * half, 128), half)] = half_mine[...].astype(F32)
        share[:, pl.ds(pl.multiple_of((1 - x) * half, 128), half)] = half_other[...].astype(F32)
        for copy in swaps + [x_first, y_first, x_second, y_second] + z_sends + [last_swap]:
            copy.wait_send()

    return [start, sum_cores, sum_first, sum_second, sum_z, finish]


SMALL_SCATTER = 6


def small_scatter_scratch():
    return [
        pltpu.VMEM((4, 2, 2, 16, 128), F32),
        pltpu.VMEM((4, 2, 16, 128), F32),
        pltpu.VMEM((4, 2, 16, 128), F32),
        pltpu.VMEM((4, 16, 128), F32),
        pltpu.VMEM((4, 16, 128), F32),
        pltpu.VMEM((3, 16, 128), F32),
        pltpu.VMEM((16, 128), F32),
        pltpu.VMEM((16, 128), F32),
        pltpu.SemaphoreType.DMA((2, SMALL_SCATTER)),
    ]


SMALL_REFS = 9


def small_scatter_steps(grads, share, bufs):
    held, pair, peer, line, from_y, z_in, mine, other, sems = bufs
    x, z, y, c = my_place()
    swap = remote(held.at[:, :, 1 - c], peer, sems, 0, place(x, z, y, 1 - c))
    to_y = remote(pair.at[:, 1 - y], from_y, sems, 1, place(x, z, 1 - y, c))
    z_sends = [
        remote(line.at[(z + k) % 4], z_in.at[k - 1], sems, 1 + k, place(x, (z + k) % 4, y, c))
        for k in (1, 2, 3)
    ]
    to_x = remote(mine, other, sems, 5, place(1 - x, z, y, c))

    def start():
        held[...] = grads[...]
        swap.start()

    def sum_cores():
        swap.wait_recv()
        pair[...] = held[:, :, c] + peer[...]
        to_y.start()

    def sum_y():
        to_y.wait_recv()
        line[...] = pair[:, y] + from_y[...]
        for copy in z_sends:
            copy.start()

    def sum_z():
        for copy in z_sends:
            copy.wait_recv()
        mine[...] = line[z] + z_in[0] + z_in[1] + z_in[2]
        to_x.start()

    def finish():
        to_x.wait_recv()
        share[...] = mine[...] + other[...]
        for copy in [swap, to_y, to_x] + z_sends:
            copy.wait_send()

    return [start, sum_cores, sum_y, sum_z, finish]


def scatter_kernel(count, small, *refs):
    total = count + small
    grads, shares = refs[:total], refs[total : 2 * total]
    scratch = refs[2 * total :]
    greet()
    plans = [
        scatter_steps(grads[i], shares[i], scratch[i * SCATTER_REFS : (i + 1) * SCATTER_REFS])
        for i in range(count)
    ]
    if small:
        plans.append(
            small_scatter_steps(grads[count], shares[count], scratch[count * SCATTER_REFS :])
        )
    for step in range(6):
        for plan in plans:
            if step < len(plan):
                plan[step]()


def scatter_call(grads, small, collective_id, name):
    count = len(grads)
    scratch, shapes = [], []
    for grad in grads:
        rows, cols = grad.shape[-2:]
        scratch += scatter_scratch(rows, cols)
        shapes.append(jax.ShapeDtypeStruct((rows, cols), F32))
    arrays = list(grads)
    in_specs = [any_spec()] * count
    if small is not None:
        arrays.append(small)
        scratch += small_scatter_scratch()
        shapes.append(jax.ShapeDtypeStruct((16, 128), F32))
        in_specs.append(pl.BlockSpec(memory_space=pltpu.VMEM))
    return pl.pallas_call(
        partial(scatter_kernel, count, int(small is not None)),
        out_shape=shapes,
        in_specs=in_specs,
        out_specs=[pl.BlockSpec(memory_space=pltpu.VMEM)] * len(shapes),
        scratch_shapes=scratch,
        compiler_params=params(collective_id=collective_id, has_side_effects=True),
        name=name,
    )(*arrays)


def mask_lanes(kind, target_row, source_row):
    places = jnp.arange(LONG, dtype=jnp.int32)
    segment = jnp.where(kind == 1, 0, places // SHORT)
    offset = jnp.where(kind == 1, places, places % SHORT)
    lane = jnp.arange(WIDE, dtype=jnp.int32) % HD
    inside = segment[:, None] == lane[None, :]
    row_side = jnp.where(inside | (lane == SEGS)[None, :], 1.0, 0.0).astype(BF16)
    picker = segment[:, None] == jnp.arange(SEGS, dtype=jnp.int32)[None, :]

    def key_side(lengths):
        live = offset < jnp.sum(jnp.where(picker, lengths[None, :], 0), axis=1)
        blocked = ((lane < SEGS)[None, :] & ~inside) | ((lane == SEGS)[None, :] & ~live[:, None])
        ones = ((lane > SEGS) & (lane < SEGS + 4))[None, :]
        return jnp.where(blocked, NEG, jnp.where(ones, 1.0, 0.0)).astype(BF16)

    return row_side, key_side(target_row), key_side(source_row)


def lower(block, row_dim):
    rows = lax.broadcasted_iota(jnp.int32, (block, block), row_dim)
    cols = lax.broadcasted_iota(jnp.int32, (block, block), 1 - row_dim)
    return cols <= rows


def attend(causal, block, q_ref, k_ref, v_ref, row_ref, key_ref, att_ref, lse_ref):
    lane = lax.broadcasted_iota(jnp.int32, (1, WIDE), 1)
    results = []
    for head in range(2):
        inside = lane // HD == head
        spare = HD * (1 - head)
        keys = jnp.where(inside, k_ref[...], key_ref[...])
        vals = jnp.where(inside, v_ref[...], jnp.where(lane == spare, 1.0, 0.0).astype(BF16))
        parts = []
        for index in range(LONG // block):
            part = pl.ds(index * block, block)
            rows = jnp.where(inside, q_ref[part, :], row_ref[part, :])
            reach = (index + 1) * block if causal else LONG
            scores = mm(rows, keys[:reach], 1, 1)
            if causal:
                edge = jnp.where(lower(block, 0), scores[:, reach - block :], NEG)
                scores = (
                    edge
                    if reach == block
                    else jnp.concatenate([scores[:, : reach - block], edge], axis=1)
                )
            top = jnp.max(scores, axis=1, keepdims=True)
            weights = jnp.exp(scores - top).astype(BF16)
            mixed = mm(weights, vals[:reach])
            total = mixed[:, spare : spare + 1]
            parts.append((mixed / total, top + jnp.log(total)))
        results.append(parts)
    for index in range(LONG // block):
        part = pl.ds(index * block, block)
        (first, lse_first), (second, lse_second) = results[0][index], results[1][index]
        att_ref[part, :] = jnp.where(lane < HD, first, second).astype(BF16)
        lse_ref[0, part, :] = jnp.where(lane == 0, lse_first, lse_second)[:, :8]


def pair_spec(offset):
    return pl.BlockSpec((LONG, WIDE), lambda i: (0, offset + i))


def lse_spec():
    return pl.BlockSpec((1, LONG, 8), lambda i: (i, 0, 0))


def attention_forward(query, keys, values, row_side, key_side, causal, name):
    return pl.pallas_call(
        partial(attend, causal, 512),
        grid=(PAIRS,),
        in_specs=[pair_spec(query[1]), pair_spec(keys[1]), pair_spec(values[1])]
        + [whole((LONG, WIDE))] * 2,
        out_specs=[pair_spec(0), lse_spec()],
        out_shape=[
            jax.ShapeDtypeStruct((LONG, D), BF16),
            jax.ShapeDtypeStruct((PAIRS, LONG, 8), F32),
        ],
        compiler_params=params(),
        cost_estimate=cost(4 * LONG * LONG * D, 8 * LONG * D, H * LONG * LONG),
        name=name,
    )(query[0], keys[0], values[0], row_side, key_side)


def three_parts(value):
    high = value.astype(BF16)
    rest = value - high.astype(F32)
    middle = rest.astype(BF16)
    return high, middle, (rest - middle.astype(F32)).astype(BF16)


def attend_back(
    causal, block, q_ref, k_ref, v_ref, att_ref, grad_ref, lse_ref, row_ref, key_ref, dq_ref, dk_ref, dv_ref
):
    lane = lax.broadcasted_iota(jnp.int32, (1, WIDE), 1)
    blocks = LONG // block
    product = att_ref[...].astype(F32) * grad_ref[...].astype(F32)
    results = []
    for head in range(2):
        inside = lane // HD == head
        spare = HD * (1 - head)
        lse_parts = three_parts(-lse_ref[0, :, head : head + 1])
        delta_parts = three_parts(
            -jnp.sum(jnp.where(inside, product, 0.0), axis=1, keepdims=True)
        )
        row_extra, grad_extra = row_ref[...], jnp.zeros((LONG, WIDE), BF16)
        for i in range(3):
            here = lane == spare + SEGS + 1 + i
            row_extra = jnp.where(here, lse_parts[i], row_extra)
            grad_extra = jnp.where(here, delta_parts[i], grad_extra)
        rows = jnp.where(inside, q_ref[...], row_extra)
        grads = jnp.where(inside, grad_ref[...], grad_extra)
        keys = jnp.where(inside, k_ref[...], key_ref[...])
        ones = (lane > spare + SEGS) & (lane < spare + SEGS + 4)
        vals = jnp.where(inside, v_ref[...], jnp.where(ones, 1.0, 0.0).astype(BF16))
        dq, dk, dv = [None] * blocks, [], []
        for index in range(blocks):
            first = index * block if causal else 0
            key_part, val_part = keys[index * block :][:block], vals[index * block :][:block]
            scores = mm(key_part, rows[first:], 1, 1)
            if causal:
                edge = jnp.where(lower(block, 1), scores[:, :block], NEG)
                scores = (
                    edge
                    if first + block == LONG
                    else jnp.concatenate([edge, scores[:, block:]], axis=1)
                )
            probs = jnp.exp(scores)
            centered = mm(val_part, grads[first:], 1, 1)
            dscores = (probs * centered).astype(BF16)
            dv.append(mm(probs.astype(BF16), grads[first:]))
            dk.append(mm(dscores, rows[first:]))
            terms = mm(dscores, key_part, 0, 0)
            for q_index in range(first // block, blocks):
                term = terms[q_index * block - first :][:block]
                dq[q_index] = term if dq[q_index] is None else dq[q_index] + term
        results.append((dq, dk, dv))
    for index in range(blocks):
        part = pl.ds(index * block, block)
        for ref, member, factor in ((dq_ref, 0, SCALE), (dk_ref, 1, 1.0), (dv_ref, 2, 1.0)):
            both = jnp.where(lane < HD, results[0][member][index], results[1][member][index])
            ref[part, :] = (both * factor).astype(BF16)


def attention_backward(query, keys, values, att, grad, lse, row_side, key_side, causal, name):
    shape = jax.ShapeDtypeStruct((LONG, D), BF16)
    return pl.pallas_call(
        partial(attend_back, causal, 256 if causal else 512),
        grid=(PAIRS,),
        in_specs=[pair_spec(query[1]), pair_spec(keys[1]), pair_spec(values[1]), pair_spec(0), pair_spec(0)]
        + [lse_spec()]
        + [whole((LONG, WIDE))] * 2,
        out_specs=[pair_spec(0)] * 3,
        out_shape=[shape] * 3,
        compiler_params=params(),
        cost_estimate=cost(10 * LONG * LONG * D, 16 * LONG * D, H * LONG * LONG),
        name=name,
    )(query[0], keys[0], values[0], att, grad, lse, row_side, key_side)


def rows_spec(block, width):
    return pl.BlockSpec((block, width), lambda i: (i, 0))


def project_in(tokens_ref, weight_ref, vec_ref, out_ref):
    mixed = mm(tokens_ref[...], weight_ref[...])
    out_ref[:, :D] = ((mixed[:, :D] + vec_ref[SELF_B : SELF_B + 1]) * SCALE).astype(BF16)
    out_ref[:, D : 2 * D] = mixed[:, D : 2 * D].astype(BF16)
    out_ref[:, 2 * D :] = (mixed[:, 2 * D :] + vec_ref[SELF_B + 1 : SELF_B + 2]).astype(BF16)


def between(
    tokens_ref, att_ref, encoded_ref, out_w, q_w, kv_w, vec_ref, resid_ref, hidden_ref, query_ref, pairs_ref
):
    pairs = mm(encoded_ref[...], kv_w[...])
    pairs_ref[:, :D] = pairs[:, :D].astype(BF16)
    pairs_ref[:, D:] = (pairs[:, D:] + vec_ref[CROSS_B + 1 : CROSS_B + 2]).astype(BF16)
    resid = tokens_ref[...].astype(F32) + mm(att_ref[...], out_w[...]) + vec_ref[SELF_B + 2 : SELF_B + 3]
    resid_ref[...] = resid
    xhat, _ = normed(resid)
    hidden = (xhat * vec_ref[GAIN : GAIN + 1] + vec_ref[SHIFT : SHIFT + 1]).astype(BF16)
    hidden_ref[...] = hidden
    query_ref[...] = ((mm(hidden, q_w[...]) + vec_ref[CROSS_B : CROSS_B + 1]) * SCALE).astype(BF16)


INV_SQRT2 = 0.7071067811865476
INV_SQRT_2PI = 0.3989422804014327


def middle(
    hidden1_ref,
    att_ref,
    cot_ref,
    cross_out,
    ffn_in,
    ffn_out,
    vec_ref,
    bias_ref,
    out_ref,
    activ_ref,
    branch3_ref,
    dpre_ref,
    hidden2_ref,
    dresid2_ref,
    branch2_ref,
    datt_ref,
    sums_ref,
    bias_sum_ref,
):
    def vec(row):
        return vec_ref[row : row + 1]

    resid2 = hidden1_ref[...].astype(F32) + mm(att_ref[...], cross_out[...]) + vec(CROSS_B + 2)
    xhat2, inv2 = normed(resid2)
    hidden2 = (xhat2 * vec(GAIN + 1) + vec(SHIFT + 1)).astype(BF16)
    hidden2_ref[...] = hidden2
    pre = mm(hidden2, ffn_in[...]) + bias_ref[...]
    phi = 0.5 + 0.5 * lax.erf(pre * INV_SQRT2)
    activ = (pre * phi).astype(BF16)
    slope = phi + pre * (INV_SQRT_2PI * jnp.exp(-0.5 * pre * pre))
    activ_ref[...] = activ
    resid3 = hidden2.astype(F32) + mm(activ, ffn_out[...]) + vec(OUT_B)
    xhat3, inv3 = normed(resid3)
    out_ref[...] = (xhat3 * vec(GAIN + 2) + vec(SHIFT + 2)).astype(BF16)
    cot = cot_ref[...].astype(F32)
    dresid3 = norm_back(xhat3, inv3, vec(GAIN + 2), cot)
    branch3 = dresid3.astype(BF16)
    branch3_ref[...] = branch3
    dpre = (mm(branch3, ffn_out[...], 1, 1) * slope).astype(BF16)
    dpre_ref[...] = dpre
    dhidden2 = dresid3 + mm(dpre, ffn_in[...], 1, 1)
    dresid2 = norm_back(xhat2, inv2, vec(GAIN + 1), dhidden2)
    dresid2_ref[...] = dresid2
    branch2 = dresid2.astype(BF16)
    branch2_ref[...] = branch2
    datt_ref[...] = mm(branch2, cross_out[...], 1, 1).astype(BF16)

    sums = jnp.concatenate(
        [
            col_sum(dhidden2 * xhat2),
            col_sum(cot * xhat3),
            col_sum(dhidden2),
            col_sum(cot),
            col_sum(branch2.astype(F32)),
            col_sum(branch3.astype(F32)),
            jnp.zeros((2, D), F32),
        ],
        axis=0,
    )
    bias_sum = col_sum(dpre.astype(F32))
    fresh = pl.program_id(0) == 0
    sums_ref[...] = jnp.where(fresh, sums, sums_ref[...] + sums)
    bias_sum_ref[...] = jnp.where(fresh, bias_sum, bias_sum_ref[...] + bias_sum)


def after_cross(
    dq_ref,
    dk_ref,
    dv_ref,
    dresid2_ref,
    resid1_ref,
    q_w,
    kv_w,
    out_w,
    vec_ref,
    encoded_grad_ref,
    dresid1_ref,
    branch1_ref,
    datt_ref,
    sums_ref,
):
    dq, dk, dv = dq_ref[...], dk_ref[...], dv_ref[...]
    encoded_grad_ref[...] = (mm(dk, kv_w[:, :D], 1, 1) + mm(dv, kv_w[:, D:], 1, 1)).astype(BF16)
    dhidden1 = dresid2_ref[...] + mm(dq, q_w[...], 1, 1)
    xhat, inv = normed(resid1_ref[...])
    dresid1 = norm_back(xhat, inv, vec_ref[GAIN : GAIN + 1], dhidden1)
    dresid1_ref[...] = dresid1
    branch1 = dresid1.astype(BF16)
    branch1_ref[...] = branch1
    datt_ref[...] = mm(branch1, out_w[...], 1, 1).astype(BF16)
    sums = jnp.concatenate(
        [
            col_sum(dhidden1 * xhat),
            col_sum(dhidden1),
            col_sum(branch1.astype(F32)),
            col_sum(dq.astype(F32)),
            col_sum(dv.astype(F32)),
            jnp.zeros((3, D), F32),
        ],
        axis=0,
    )
    sums_ref[...] = jnp.where(pl.program_id(0) == 0, sums, sums_ref[...] + sums)


def tokens_back(dq_ref, dk_ref, dv_ref, dresid1_ref, weight_ref, out_ref):
    total = dresid1_ref[...] + mm(dq_ref[...], weight_ref[:, :D], 1, 1)
    total = total + mm(dk_ref[...], weight_ref[:, D : 2 * D], 1, 1)
    out_ref[...] = (total + mm(dv_ref[...], weight_ref[:, 2 * D :], 1, 1)).astype(BF16)


def row_call(kernel, block, ins, weights, outs, sums, name, flops):
    in_specs = [rows_spec(block, a.shape[1]) for a in ins]
    for _, shape, index in weights:
        in_specs.append(pl.BlockSpec(shape, lambda i, index=index: index))
    out_specs = [rows_spec(block, width) for width, _ in outs] + [whole(s) for s in sums]
    out_shape = [jax.ShapeDtypeStruct((LONG, width), dtype) for width, dtype in outs]
    out_shape += [jax.ShapeDtypeStruct(s, F32) for s in sums]
    return pl.pallas_call(
        kernel,
        grid=(LONG // block,),
        in_specs=in_specs,
        out_specs=out_specs,
        out_shape=out_shape,
        compiler_params=params(),
        cost_estimate=cost(flops, flops / 500),
        name=name,
    )(*ins, *[w[0] for w in weights])


def ffn_grads(activ_ref, branch3_ref, hidden2_ref, dpre_ref, out_grad_ref, in_grad_ref):
    out_grad_ref[...] = mm(activ_ref[...], branch3_ref[...], 0, 0).astype(BF16)
    in_grad_ref[...] = mm(hidden2_ref[...], dpre_ref[...], 0, 0).astype(BF16)


def ffn_grads_call(activ, branch3, hidden2, dpre):
    tile = 512
    return pl.pallas_call(
        ffn_grads,
        grid=(FF // tile,),
        in_specs=[
            pl.BlockSpec((LONG, tile), lambda i: (0, i)),
            whole((LONG, D)),
            whole((LONG, D)),
            pl.BlockSpec((LONG, tile), lambda i: (0, i)),
        ],
        out_specs=[
            pl.BlockSpec((tile, D), lambda i: (i, 0)),
            pl.BlockSpec((D, tile), lambda i: (0, i)),
        ],
        out_shape=[jax.ShapeDtypeStruct((FF, D), BF16), jax.ShapeDtypeStruct((D, FF), BF16)],
        compiler_params=params(),
        cost_estimate=cost(4 * LONG * D * FF, 8 * LONG * FF),
        name="ffn_grads",
    )(activ, branch3, hidden2, dpre)


def pair_grads(count, *refs):
    out_ref = refs[2 * count]
    for index in range(count):

        @pl.when(pl.program_id(0) == index)
        def _(index=index):
            out_ref[...] = mm(refs[index][...], refs[count + index][...], 0, 0).astype(BF16)


def pair_grads_call(lefts, rights, name):
    count = len(lefts)
    return pl.pallas_call(
        partial(pair_grads, count),
        grid=(count,),
        in_specs=[whole((LONG, D))] * (2 * count),
        out_specs=pl.BlockSpec((D, D), lambda i: (0, i)),
        out_shape=jax.ShapeDtypeStruct((D, D * count), BF16),
        compiler_params=params(),
        cost_estimate=cost(2 * LONG * D * D * count, 4 * LONG * D * count),
        name=name,
    )(*lefts, *rights)


def body(
    tokens,
    encoded,
    cotangent,
    bucket,
    target_len,
    source_len,
    self_in,
    self_bias,
    self_out,
    cross_q,
    cross_kv,
    cross_bias,
    cross_out,
    ffn_in,
    ffn_in_bias,
    ffn_out,
    ffn_out_bias,
    norm_gain,
    norm_shift,
):
    rows = self_in.shape[0]
    owners = D // rows
    direct = owners == 16
    row_side, target_side, source_side = mask_lanes(bucket[0], target_len[0], source_len[0])

    small = jnp.concatenate(
        [
            self_bias.reshape(-1),
            cross_bias.reshape(-1),
            norm_gain.reshape(-1),
            norm_shift.reshape(-1),
            ffn_out_bias,
            ffn_in_bias,
        ]
    )
    mixed_w = jnp.concatenate([self_out, cross_q, cross_kv, cross_out], axis=1)
    if direct:
        small = jnp.pad(small, (0, PACK - small.shape[0])).reshape(16, 128)
        self_w, small_all = gather_call([self_in], small, 0, "gather_self")
        (mixed_w,) = gather_call([mixed_w], None, 1, "gather_cross")
        ffn_in_w, ffn_out_w = gather_call([ffn_in, ffn_out], None, 2, "gather_ffn")
        small_all = small_all.reshape(16, PACK)
    else:
        everyone = partial(lax.all_gather, axis_name="fsdp", axis=0, tiled=True)
        self_w, mixed_w, ffn_in_w, ffn_out_w = map(everyone, (self_in, mixed_w, ffn_in, ffn_out))
        small_all = lax.all_gather(small, "fsdp", axis=0, tiled=False)
    self_w, mixed_w = self_w.reshape(D, 3 * D), mixed_w.reshape(D, 5 * D)
    ffn_in_w, ffn_out_w = ffn_in_w.reshape(D, FF), ffn_out_w.reshape(FF, D)
    small_all = small_all.astype(F32)
    vec = small_all[:, : IN_B * rows].reshape(owners, IN_B, rows).transpose(1, 0, 2).reshape(IN_B, D)
    vec = jnp.pad(vec, ((0, 3), (0, 0)))
    bias = small_all[:, IN_B * rows : VEC_ROWS * rows].reshape(1, FF)
    vec_weight = (vec, (16, D), (0, 0))
    square = (D, D)

    (mixed,) = row_call(
        project_in,
        512,
        [tokens],
        [(self_w, (D, 3 * D), (0, 0)), vec_weight],
        [(3 * D, BF16)],
        [],
        "project_in",
        6 * LONG * D * D,
    )
    self_att, self_lse = attention_forward(
        (mixed, 0), (mixed, PAIRS), (mixed, 2 * PAIRS), row_side, target_side, True, "self_forward"
    )
    resid1, hidden1, query, pairs = row_call(
        between,
        512,
        [tokens, self_att, encoded],
        [(mixed_w, square, (0, 0)), (mixed_w, square, (0, 1)), (mixed_w, (D, 2 * D), (0, 1)), vec_weight],
        [(D, F32), (D, BF16), (D, BF16), (2 * D, BF16)],
        [],
        "between",
        8 * LONG * D * D,
    )
    cross_att, cross_lse = attention_forward(
        (query, 0), (pairs, 0), (pairs, PAIRS), row_side, source_side, False, "cross_forward"
    )
    (output, activ, branch3, dpre, hidden2, dresid2, branch2, d_cross_att, sums_mid, bias_sum) = row_call(
        middle,
        256,
        [hidden1, cross_att, cotangent],
        [
            (mixed_w, square, (0, 4)),
            (ffn_in_w, (D, FF), (0, 0)),
            (ffn_out_w, (FF, D), (0, 0)),
            vec_weight,
            (bias, (1, FF), (0, 0)),
        ],
        [(D, BF16), (FF, BF16), (D, BF16), (FF, BF16), (D, BF16), (D, F32), (D, BF16), (D, BF16)],
        [(8, D), (1, FF)],
        "middle",
        36 * LONG * D * D,
    )
    ffn_out_grad, ffn_in_grad = ffn_grads_call(activ, branch3, hidden2, dpre)
    dcq, dck, dcv = attention_backward(
        (query, 0),
        (pairs, 0),
        (pairs, PAIRS),
        cross_att,
        d_cross_att,
        cross_lse,
        row_side,
        source_side,
        False,
        "cross_backward",
    )
    encoded_grad, dresid1, branch1, d_self_att, sums_cross = row_call(
        after_cross,
        512,
        [dcq, dck, dcv, dresid2, resid1],
        [(mixed_w, square, (0, 1)), (mixed_w, (D, 2 * D), (0, 1)), (mixed_w, square, (0, 0)), vec_weight],
        [(D, BF16), (D, F32), (D, BF16), (D, BF16)],
        [(8, D)],
        "after_cross",
        8 * LONG * D * D,
    )
    mixed_grad = pair_grads_call(
        [self_att, hidden1, encoded, encoded, cross_att],
        [branch1, dcq, dck, dcv, branch2],
        "cross_grads",
    )
    dq, dk, dv = attention_backward(
        (mixed, 0),
        (mixed, PAIRS),
        (mixed, 2 * PAIRS),
        self_att,
        d_self_att,
        self_lse,
        row_side,
        target_side,
        True,
        "self_backward",
    )
    self_grad = pair_grads_call([tokens] * 3, [dq, dk, dv], "self_grads")
    (tokens_grad,) = row_call(
        tokens_back,
        512,
        [dq, dk, dv, dresid1],
        [(self_w, (D, 3 * D), (0, 0))],
        [(D, BF16)],
        [],
        "tokens_back",
        6 * LONG * D * D,
    )

    dq_sum = jnp.sum(dq.astype(F32), axis=0, keepdims=True)
    dv_sum = jnp.sum(dv.astype(F32), axis=0, keepdims=True)
    small_rows = jnp.concatenate(
        [
            dq_sum,
            dv_sum,
            sums_cross[2:5],
            sums_mid[4:5],
            sums_cross[0:1],
            sums_mid[0:2],
            sums_cross[1:2],
            sums_mid[2:4],
            sums_mid[5:6],
        ],
        axis=0,
    )
    packed = small_rows.reshape(IN_B, owners, rows).transpose(1, 0, 2).reshape(owners, IN_B * rows)
    packed = jnp.concatenate([packed, bias_sum.reshape(owners, 4 * rows)], axis=1)
    grads = [self_grad, mixed_grad, ffn_in_grad, ffn_out_grad]
    if direct:
        packed = jnp.pad(packed, ((0, 0), (0, PACK - packed.shape[1]))).reshape(4, 2, 2, 16, 128)

        def cut(grad):
            return grad.reshape(4, 2, 2, grad.shape[0] // 16, grad.shape[1])

        ffn_in_share, ffn_out_share = scatter_call(
            [cut(ffn_in_grad), cut(ffn_out_grad)], None, 3, "scatter_ffn"
        )
        (mixed_share,) = scatter_call([cut(mixed_grad)], None, 4, "scatter_cross")
        self_share, packed_share = scatter_call([cut(self_grad)], packed, 5, "scatter_self")
        packed_share = packed_share.reshape(-1)
    else:

        def share_of(grad):
            share = lax.psum_scatter(grad.astype(F32), "fsdp", scatter_dimension=0, tiled=True)
            return lax.psum(share, "dp")

        self_share, mixed_share, ffn_in_share, ffn_out_share = map(share_of, grads)
        packed_share = share_of(packed).reshape(-1)

    def rows_of(first, count):
        return packed_share[first * rows : (first + count) * rows]

    return (
        output,
        tokens_grad,
        encoded_grad,
        self_share,
        rows_of(SELF_B, 3).reshape(3, rows),
        mixed_share[:, :D],
        mixed_share[:, D : 2 * D],
        mixed_share[:, 2 * D : 4 * D],
        rows_of(CROSS_B, 3).reshape(3, rows),
        mixed_share[:, 4 * D :],
        ffn_in_share,
        rows_of(IN_B, 4),
        ffn_out_share,
        rows_of(OUT_B, 1),
        rows_of(GAIN, 3).reshape(3, rows),
        rows_of(SHIFT, 3).reshape(3, rows),
    )


def solution(mesh):
    both = P(("dp", "fsdp"), None)
    rows, cols, flat = P("fsdp", None), P(None, "fsdp"), P("fsdp")
    return jax.shard_map(
        body,
        mesh=mesh,
        in_specs=(both, both, both, P(("dp", "fsdp")), both, both)
        + (rows, cols, rows, rows, rows, cols, rows, rows, flat, rows, flat, cols, cols),
        out_specs=(both, both, both)
        + (rows, cols, rows, rows, rows, cols, rows, rows, flat, rows, flat, cols, cols),
        check_vma=False,
    )
```

time: 1460 us -> 587 us (0.40)
  Pallas kernels: 0 us -> 547 us
  matrix products: 457 us -> 0 us
  waiting for transfers between devices: 381 us -> 0 us
  blocking collectives: 218 us -> 0 us
  other arithmetic: 193 us -> 6.91 us
  local copies, waits for them, and re-layouts: 173 us -> 22.1 us
  between operations: 22 us -> 2.01 us
    pallas_call x0 -> x18, Pallas kernels: none -> 547 us  [the longest x3 180 us: scatter_call(): pl.pallas_call(partial(scatter_kernel, count, int(small is not None)), ou...]
    dot_general x66 -> x0, matrix products: 457 us -> none  [the longest x7 86.5 us: block_dprobs(): jnp.einsum('qhd,khd->hqk', grad_rows, vals, preferred_element_type=jnp.fl...]
    reduce_scatter x12 -> x0, waiting for transfers between devices: 195 us -> none  [the longest x1 109 us: body(): lax.psum_scatter(ffn_members[2], 'fsdp', scatter_dimension=0, tiled=True)]
    unnamed x27 -> x0, waiting for transfers between devices: 186 us -> none
    convert_element_type x34 -> x2, other arithmetic: 134 us -> 2.5 us  [the longest x1 1.6 us: key_side(): return jnp.where(blocked, NEG, jnp.where(ones, 1.0, 0.0)).astype(BF16)]
    unnamed x4 -> x0, blocking collectives: 131 us -> none
    all_gather x11 -> x0, blocking collectives: 87.6 us -> none  [the longest x1 23.4 us: body(): lax.all_gather(self_bias, 'fsdp', axis=1, tiled=True)]
    cond x24 -> x0, local copies, waits for them, and re-layouts: 77.6 us -> none  [the longest x6 76.2 us: maybe(): return lax.cond(active, compute, empty)]
  transfers between devices with their start and end apart: 23 -> 0, of which waited for: 11 -> 0; matrix products, arithmetic and copies ran while one was open for 49% -> 0% of each run, Pallas kernels for 0% -> 0%
where the time goes in v1:
time: 587 us; the launch traced here: 578 us
  Pallas kernels  547 us (93%)
  local copies, waits for them, and re-layouts  22.1 us (4%)
  other arithmetic  6.91 us (1%)
    pallas_call x3, Pallas kernels, scatter_call(): pl.pallas_call(partial(scatter_kernel, count, int(small is not None)), ou...  180 us
    pallas_call x3, Pallas kernels, gather_call(): pl.pallas_call(partial(gather_kernel, count, has_small), out_shape=[gathe...  140 us
    pallas_call x5, Pallas kernels, row_call(): pl.pallas_call(kernel, grid=(LONG // block,), in_specs=in_specs, out_spec...  78.1 us
    pallas_call x2, Pallas kernels, attention_backward(): pl.pallas_call(partial(attend_back, causal, 256 if causal else 512), grid...  67.2 us
    pallas_call x2, Pallas kernels, attention_forward(): pl.pallas_call(partial(attend, causal, 512), grid=(PAIRS,), in_specs=[pai...  42.5 us
    pallas_call x2, Pallas kernels, pair_grads_call(): pl.pallas_call(partial(pair_grads, count), grid=(count,), in_specs=[whole...  24.2 us
    pallas_call x1, Pallas kernels, ffn_grads_call(): pl.pallas_call(ffn_grads, grid=(FF // tile,), in_specs=[pl.BlockSpec((LON...  14.7 us

profile of v1, /device:TPU:0, one launch (start us, length us, event | category | flops | bytes accessed | tf_op | source)
XLA Modules:
  0.0 578.0 jit_solution(9389631609202954133)
XLA Ops:
  1.3 0.8 select_reduce_fusion
  2.1 1.6 select_convert_fusion
  3.7 0.9 select_convert_fusion.2.row_ref
  4.6 0.8 reshape.180
  5.4 0.8 reshape.181
  6.2 0.8 reshape.182
  6.9 0.8 reshape.183
  7.7 1.4 concatenate.31
  9.1 0.6 pad_bitcast_fusion.refs_1_
  9.7 34.8 %gather_self.1 = (bf16[4,2,2,48,2304]{4,3,2,1,0:T(8,128)(2,1)}, bf16[4,2,2,16,128]{4,3,2,1,0:T(8,128)(2,1)}) custom-call(bf16[48,2304]{1,0:T(8,128)(2,1)} %refs_0_.3, bf16[16,128]{1,0:T(8,128)(2,1)} %pad_bitcast_fusion.refs_1_), custom_call_target="tpu_custom_call" | custom-call | tf_op jit(solution)/shard_map/gather_self/pallas_call | solution.py:246
  44.5 0.9 copy.55
  45.4 0.1 reshape.186
  45.6 0.1 reshape.187
  45.7 0.6 pad.13.vec_ref
  46.3 7.7 %project_in.1.q_ref.k_ref.v_ref = bf16[1024,2304]{1,0:T(8,128)(2,1)} custom-call(bf16[1024,768]{1,0:T(8,128)(2,1)} %refs_2_.2, bf16[768,2304]{1,0:T(8,128)(2,1)} %bitcast.58, f32[16,768]{1,0:T(8,128)} %pad.13.vec_ref), custom_call_target="tpu_custom_call" | custom-call | flops 3623878656 | bytes 7247757 | tf_op jit(solution)/shard_map/project_in/pallas_call | solution.py:785
  54.0 19.0 %self_forward.1 = (bf16[1024,768]{1,0:T(8,128)(2,1)}, f32[6,1024,8]{2,1,0:T(8,128)}) custom-call(bf16[1024,2304]{1,0:T(8,128)(2,1)} %project_in.1.q_ref.k_ref.v_ref, bf16[1024,2304]{1,0:T(8,128)(2,1)} %project_in.1.q_ref.k_ref.v_ref, bf16[1024,2304]{1,0:T(8,128)(2,1)} %project_in.1.q_ref.k_ref.v_ref, bf16[1024,128]{1,0:T(8,128)(2,1)} %select_convert_fusion.2.row_ref, ...), custom_call_target="tpu_custom_call" | custom-call | flops 3221225472 | bytes 6291456 | tf_op jit(solution)/shard_map/self_forward/pallas_call | solution.py:546
  73.1 0.8 pad_maximum_fusion.refs_0_
  73.8 45.3 %gather_cross.1 = bf16[4,2,2,48,3840]{4,3,2,1,0:T(8,128)(2,1)} custom-call(bf16[48,3840]{1,0:T(8,128)(2,1)} %pad_maximum_fusion.refs_0_), custom_call_target="tpu_custom_call" | custom-call | tf_op jit(solution)/shard_map/gather_cross/pallas_call | solution.py:246
  119.1 11.2 %between.1 = (f32[1024,768]{1,0:T(8,128)}, bf16[1024,768]{1,0:T(8,128)(2,1)}, bf16[1024,768]{1,0:T(8,128)(2,1)}, bf16[1024,1536]{1,0:T(8,128)(2,1)}) custom-call(bf16[1024,768]{1,0:T(8,128)(2,1)} %refs_2_.2, bf16[1024,768]{1,0:T(8,128)(2,1)} %get-tuple-element.57.att_ref.refs_0_, bf16[1024,768]{1,0:T(8,128)(2,1)} %refs_3_.1, bf16[768,3840]{1,0:T(8,128)(2,1)} %bitcast.30, ...), custom_call_target="tpu_custom_call" | custom-call | flops 4831838208 | bytes 9663676 | tf_op jit(solution)/shard_map/between/pallas_call | solution.py:785
  130.4 23.4 %cross_forward.1 = (bf16[1024,768]{1,0:T(8,128)(2,1)}, f32[6,1024,8]{2,1,0:T(8,128)}) custom-call(bf16[1024,768]{1,0:T(8,128)(2,1)} %get-tuple-element.59.q_ref, bf16[1024,1536]{1,0:T(8,128)(2,1)} %get-tuple-element.60.k_ref.v_ref, bf16[1024,1536]{1,0:T(8,128)(2,1)} %get-tuple-element.60.k_ref.v_ref, bf16[1024,128]{1,0:T(8,128)(2,1)} %select_convert_fusion.2.row_ref, ...), custom_call_target="tpu_custom_call" | custom-call | flops 3221225472 | bytes 6291456 | tf_op jit(solution)/shard_map/cross_forward/pallas_call | solution.py:546
  153.8 0.1 slice.77
  153.9 0.7 reshape.191.bias_ref
  154.6 59.9 %gather_ffn.1 = (bf16[4,2,2,48,3072]{4,3,2,1,0:T(8,128)(2,1)}, bf16[4,2,2,192,768]{4,3,2,1,0:T(8,128)(2,1)}) custom-call(bf16[48,3072]{1,0:T(8,128)(2,1)} %refs_0_.4, bf16[192,768]{1,0:T(8,128)(2,1)} %refs_1_.2), custom_call_target="tpu_custom_call" | custom-call | tf_op jit(solution)/shard_map/gather_ffn/pallas_call | solution.py:246
  214.5 37.5 %middle.1 = (bf16[1024,768]{1,0:T(8,128)(2,1)}, bf16[1024,3072]{1,0:T(8,128)(2,1)}, bf16[1024,768]{1,0:T(8,128)(2,1)}, bf16[1024,3072]{1,0:T(8,128)(2,1)}, bf16[...) custom-call(bf16[1024,768]{1,0:T(8,128)(2,1)} %get-tuple-element.58., ...), custom_call_target="tpu_custom_call" | custom-call | flops 21743271936 | bytes 43486544 | tf_op jit(solution)/shard_map/middle/pallas_call | solution.py:785
  251.9 14.7 %ffn_grads.1 = (bf16[3072,768]{1,0:T(8,128)(2,1)}, bf16[768,3072]{1,0:T(8,128)(2,1)}) custom-call(bf16[1024,3072]{1,0:T(8,128)(2,1)} %get-tuple-element.86.activ_ref, bf16[1024,768]{1,0:T(8,128)(2,1)} %get-tuple-element.87.branch3_ref, bf16[1024,768]{1,0:T(8,128)(2,1)} %get-tuple-element.88.hidden2_ref, bf16[1024,3072]{1,0:T(8,128)(2,1)} %get-tuple-element.89.dpre_ref), custom_call_target="tpu_custom_call" | custom-call | flops 9663676416 | bytes 25165824 | tf_op jit(solution)/shard_map/ffn_grads/pallas_call | solution.py:804
  266.7 80.3 %scatter_ffn.1 = (f32[48,3072]{1,0:T(8,128)}, f32[192,768]{1,0:T(8,128)}) custom-call(bf16[4,2,2,48,3072]{4,3,2,1,0:T(8,128)(2,1)} %bitcast.39, bf16[4,2,2,192,768]{4,3,2,1,0:T(8,128)(2,1)} %bitcast.38), custom_call_target="tpu_custom_call" | custom-call | tf_op jit(solution)/shard_map/scatter_ffn/pallas_call | solution.py:468
  347.0 39.2 %cross_backward.1 = (bf16[1024,768]{1,0:T(8,128)(2,1)}, bf16[1024,768]{1,0:T(8,128)(2,1)}, bf16[1024,768]{1,0:T(8,128)(2,1)}) custom-call(bf16[1024,768]{1,0:T(8,128)(2,1)} %get-tuple-element.59.q_ref, bf16[1024,1536]{1,0:T(8,128)(2,1)} %get-tuple-element.60.k_ref.v_ref, bf16[1024,1536]{1,0:T(8,128)(2,1)} %get-tuple-element.60.k_ref.v_ref, ...), custom_call_target="tpu_custom_call" | custom-call | flops 8053063680 | bytes 12582912 | tf_op jit(solution)/shard_map/cross_backward/pallas_call | solution.py:624
  386.1 13.0 %after_cross.1 = (bf16[1024,768]{1,0:T(8,128)(2,1)}, f32[1024,768]{1,0:T(8,128)}, bf16[1024,768]{1,0:T(8,128)(2,1)}, bf16[1024,768]{1,0:T(8,128)(2,1)}, f32[8,768]{1,0:T(8,128)}) custom-call(bf16[1024,768]{1,0:T(8,128)(2,1)} %get-tuple-element.67.dq_ref.refs_6_, bf16[1024,768]{1,0:T(8,128)(2,1)} %get-tuple-element.68.dk_ref.refs_7_, ...), custom_call_target="tpu_custom_call" | custom-call | flops 4831838208 | bytes 9663676 | tf_op jit(solution)/shard_map/after_cross/pallas_call | solution.py:785
  399.1 14.3 %cross_grads.1 = bf16[768,3840]{1,0:T(8,128)(2,1)} custom-call(bf16[1024,768]{1,0:T(8,128)(2,1)} %get-tuple-element.57.att_ref.refs_0_, bf16[1024,768]{1,0:T(8,128)(2,1)} %get-tuple-element.58.hidden1_ref.refs_1_, bf16[1024,768]{1,0:T(8,128)(2,1)} %refs_3_.1, bf16[1024,768]{1,0:T(8,128)(2,1)} %refs_3_.1, ...), custom_call_target="tpu_custom_call" | custom-call | flops 6039797760 | bytes 15728640 | tf_op jit(solution)/shard_map/cross_grads/pallas_call | solution.py:835
  413.4 55.3 %scatter_cross.1 = f32[48,3840]{1,0:T(8,128)} custom-call(bf16[4,2,2,48,3840]{4,3,2,1,0:T(8,128)(2,1)} %bitcast.37), custom_call_target="tpu_custom_call" | custom-call | tf_op jit(solution)/shard_map/scatter_cross/pallas_call | solution.py:468
  468.7 1.8 fusion.15
  470.5 1.7 slice.69
  472.2 28.0 %self_backward.1 = (bf16[1024,768]{1,0:T(8,128)(2,1)}, bf16[1024,768]{1,0:T(8,128)(2,1)}, bf16[1024,768]{1,0:T(8,128)(2,1)}) custom-call(bf16[1024,2304]{1,0:T(8,128)(2,1)} %project_in.1.q_ref.k_ref.v_ref, bf16[1024,2304]{1,0:T(8,128)(2,1)} %project_in.1.q_ref.k_ref.v_ref, bf16[1024,2304]{1,0:T(8,128)(2,1)} %project_in.1.q_ref.k_ref.v_ref, ...), custom_call_target="tpu_custom_call" | custom-call | flops 8053063680 | bytes 12582912 | tf_op jit(solution)/shard_map/self_backward/pallas_call | solution.py:624
  500.2 1.8 convert_reduce_fusion.1
  502.0 0.1 concatenate.33
  502.1 0.3 convert_reduce_fusion
  502.4 0.1 concatenate.34
  502.5 0.1 concatenate.35
  502.7 0.1 concatenate.37
  502.7 0.1 concatenate.39
  502.8 0.1 concatenate.38
  502.9 0.1 concatenate.40
  503.1 0.1 concatenate.36
  503.1 0.1 concatenate.41
  503.2 0.3 concatenate.42
  503.5 0.1 reshape.193
  503.6 0.5 broadcast.195
  504.1 0.7 reduce.11
  504.8 0.1 reshape.194
  504.8 0.1 fusion.1
  504.9 0.7 copy.53
  505.6 9.9 %self_grads.1 = bf16[768,2304]{1,0:T(8,128)(2,1)} custom-call(bf16[1024,768]{1,0:T(8,128)(2,1)} %refs_2_.2, bf16[1024,768]{1,0:T(8,128)(2,1)} %refs_2_.2, bf16[1024,768]{1,0:T(8,128)(2,1)} %refs_2_.2, bf16[1024,768]{1,0:T(8,128)(2,1)} %get-tuple-element.74.dq_ref.refs_3_, bf16[1024,768]{1,0:T(8,128)(2,1)} %get-tuple-element.75.dk_ref.refs_4_, ...), custom_call_target="tpu_custom_call" | custom-call | flops 3623878656 | bytes 9437184 | tf_op jit(solution)/shard_map/self_grads/pallas_call | solution.py:835
  515.5 44.8 %scatter_self.1 = (f32[48,2304]{1,0:T(8,128)}, f32[16,128]{1,0:T(8,128)}) custom-call(bf16[4,2,2,48,2304]{4,3,2,1,0:T(8,128)(2,1)} %bitcast.40, f32[4,2,2,16,128]{4,3,2,1,0:T(8,128)} %bitcast.41), custom_call_target="tpu_custom_call" | custom-call | tf_op jit(solution)/shard_map/scatter_self/pallas_call | solution.py:468
  560.2 0.9 fusion.17
  561.2 0.7 reshape.197
  561.8 0.7 reshape.199
  562.5 0.7 reshape.202
  563.1 0.7 reshape.203
  563.8 1.3 slice.80
  565.1 1.3 slice.81
  566.4 8.7 %tokens_back.1 = bf16[1024,768]{1,0:T(8,128)(2,1)} custom-call(bf16[1024,768]{1,0:T(8,128)(2,1)} %get-tuple-element.74.dq_ref.refs_3_, bf16[1024,768]{1,0:T(8,128)(2,1)} %get-tuple-element.75.dk_ref.refs_4_, bf16[1024,768]{1,0:T(8,128)(2,1)} %get-tuple-element.76.dv_ref.refs_5_, f32[1024,768]{1,0:T(8,128)} %get-tuple-element.77.dresid1_ref, ...), custom_call_target="tpu_custom_call" | custom-call | flops 3623878656 | bytes 7247757 | tf_op jit(solution)/shard_map/tokens_back/pallas_call | solution.py:785
  575.1 0.8 copy.60
  575.9 0.8 copy.61
  576.7 0.8 copy.62
  (36 shorter events, 0.2 us)
Async XLA Ops:
  54.0 19.1 %copy-start.4 = (bf16[48,1536]{1,0:T(8,128)(2,1)S(1)}, bf16[48,1536]{1,0:T(8,128)(2,1)}, u32[]{:S(2)}) copy-start(bf16[48,1536]{1,0:T(8,128)(2,1)} %param.29) | copy-start | bytes 442372
  54.0 19.1 %copy-start.5 = (bf16[48,768]{1,0:T(8,128)(2,1)S(1)}, bf16[48,768]{1,0:T(8,128)(2,1)}, u32[]{:S(2)}) copy-start(bf16[48,768]{1,0:T(8,128)(2,1)} %param.31) | copy-start | bytes 221188
  54.0 19.1 %copy-start.6 = (bf16[48,768]{1,0:T(8,128)(2,1)S(1)}, bf16[48,768]{1,0:T(8,128)(2,1)}, u32[]{:S(2)}) copy-start(bf16[48,768]{1,0:T(8,128)(2,1)} %param.28) | copy-start | bytes 221188
  54.0 19.1 %copy-start.7 = (bf16[48,768]{1,0:T(8,128)(2,1)S(1)}, bf16[48,768]{1,0:T(8,128)(2,1)}, u32[]{:S(2)}) copy-start(bf16[48,768]{1,0:T(8,128)(2,1)} %param.27) | copy-start | bytes 221188
  500.2 1.9 copy-start
  500.2 2.3 copy-start.9
  500.2 2.6 copy-start.8
  502.0 2.1 copy-start.10
  566.4 8.7 %copy-start.3 = (f32[48,2304]{1,0:T(8,128)S(1)}, f32[48,2304]{1,0:T(8,128)}, u32[]{:S(2)}) copy-start(f32[48,2304]{1,0:T(8,128)} %get-tuple-element.134) | copy-start | bytes 1327108
  566.4 9.5 %copy-start.2 = (f32[48,3072]{1,0:T(8,128)S(1)}, f32[48,3072]{1,0:T(8,128)}, u32[]{:S(2)}) copy-start(f32[48,3072]{1,0:T(8,128)} %get-tuple-element.141) | copy-start | bytes 1769476
  575.1 1.6 copy-start.1

commit v2 on v1

--- a/solution.py
+++ b/solution.py
@@ -23,7 +23,7 @@
 F32 = jnp.float32
 BF16 = jnp.bfloat16
 MESH_ID = pl.DeviceIdType.MESH
-VMEM_LIMIT = 56 << 20
+VMEM_LIMIT = 60 << 20
 
 SELF_B, CROSS_B, GAIN, SHIFT, OUT_B, IN_B = 0, 3, 6, 9, 12, 13
 VEC_ROWS = 17
@@ -111,7 +111,7 @@
 
 def gather_copies(shard, full, sems, local_sem):
     x, z, y, c = my_place()
-    half = shard.shape[1] // 2
+    half = shard.shape[-1] // 2
     mine = pl.ds(pl.multiple_of(x * half, 128), half)
     other = pl.ds(pl.multiple_of((1 - x) * half, 128), half)
     to_x, to_y, to_c = place(1 - x, z, y, c), place(x, z, 1 - y, c), place(x, z, y, 1 - c)
@@ -164,13 +164,15 @@
         copies[6].wait_recv()
         copies[10].start()
 
-    def last():
+    def arrive():
         for index in (7, 8, 9, 10):
             copies[index].wait_recv()
+
+    def last():
         for copy in copies:
             copy.wait_send()
 
-    return [first, second, third, fourth, last]
+    return [first, second, third, fourth, arrive, last]
 
 
 SMALL_COPIES = 5
@@ -200,58 +202,18 @@
         copies[3].wait_recv()
         copies[4].start()
 
+    def fourth():
+        copies[4].wait_recv()
+
     def last():
-        copies[4].wait_recv()
         for copy in copies:
             copy.wait_send()
 
-    return [first, second, third, last]
-
-
-def gather_kernel(count, small, *refs):
-    total = count + small
-    shards, fulls = refs[:total], refs[total : 2 * total]
-    sems = refs[2 * total :]
-    greet()
-    plans = [
-        gather_steps(shards[i], fulls[i], sems[2 * i], sems[2 * i + 1].at[0]) for i in range(count)
-    ]
-    if small:
-        plans.append(
-            small_gather_steps(shards[count], fulls[count], sems[2 * count], sems[2 * count + 1].at[0])
-        )
-    for step in range(5):
-        for plan in plans:
-            if step < len(plan):
-                plan[step]()
-
-
-def gather_scratch(count, small):
-    scratch = []
-    for _ in range(count):
-        scratch += [pltpu.SemaphoreType.DMA((2, GATHER_COPIES)), pltpu.SemaphoreType.DMA((1,))]
-    if small:
-        scratch += [pltpu.SemaphoreType.DMA((2, SMALL_COPIES)), pltpu.SemaphoreType.DMA((1,))]
-    return scratch
-
-
-def gather_shape(shard):
-    return jax.ShapeDtypeStruct((4, 2, 2) + shard.shape, shard.dtype)
-
-
-def gather_call(shards, small, collective_id, name):
-    count = len(shards)
-    arrays = list(shards) + ([small] if small is not None else [])
-    has_small = int(small is not None)
-    return pl.pallas_call(
-        partial(gather_kernel, count, has_small),
-        out_shape=[gather_shape(a) for a in arrays],
-        in_specs=[any_spec()] * len(arrays),
-        out_specs=[any_spec()] * len(arrays),
-        scratch_shapes=gather_scratch(count, has_small),
-        compiler_params=params(collective_id=collective_id, has_side_effects=True),
-        name=name,
-    )(*arrays)
+    return [first, second, third, fourth, last]
+
+
+def gather_shape(rows, cols):
+    return (4, 2, 2, rows, cols)
 
 
 SCATTER_COPIES = 10
@@ -639,11 +601,11 @@
     return pl.BlockSpec((block, width), lambda i: (i, 0))
 
 
-def project_in(tokens_ref, weight_ref, vec_ref, out_ref):
-    mixed = mm(tokens_ref[...], weight_ref[...])
-    out_ref[:, :D] = ((mixed[:, :D] + vec_ref[SELF_B : SELF_B + 1]) * SCALE).astype(BF16)
-    out_ref[:, D : 2 * D] = mixed[:, D : 2 * D].astype(BF16)
-    out_ref[:, 2 * D :] = (mixed[:, 2 * D :] + vec_ref[SELF_B + 1 : SELF_B + 2]).astype(BF16)
+def project_in(tokens_ref, q_w, k_w, v_w, vec_ref, out_ref):
+    left = tokens_ref[...]
+    out_ref[:, :D] = ((mm(left, q_w[...]) + vec_ref[SELF_B : SELF_B + 1]) * SCALE).astype(BF16)
+    out_ref[:, D : 2 * D] = mm(left, k_w[...]).astype(BF16)
+    out_ref[:, 2 * D :] = (mm(left, v_w[...]) + vec_ref[SELF_B + 1 : SELF_B + 2]).astype(BF16)
 
 
 def between(
@@ -769,10 +731,10 @@
     sums_ref[...] = jnp.where(pl.program_id(0) == 0, sums, sums_ref[...] + sums)
 
 
-def tokens_back(dq_ref, dk_ref, dv_ref, dresid1_ref, weight_ref, out_ref):
-    total = dresid1_ref[...] + mm(dq_ref[...], weight_ref[:, :D], 1, 1)
-    total = total + mm(dk_ref[...], weight_ref[:, D : 2 * D], 1, 1)
-    out_ref[...] = (total + mm(dv_ref[...], weight_ref[:, 2 * D :], 1, 1)).astype(BF16)
+def tokens_back(dq_ref, dk_ref, dv_ref, dresid1_ref, q_w, k_w, v_w, out_ref):
+    total = dresid1_ref[...] + mm(dq_ref[...], q_w[...], 1, 1)
+    total = total + mm(dk_ref[...], k_w[...], 1, 1)
+    out_ref[...] = (total + mm(dv_ref[...], v_w[...], 1, 1)).astype(BF16)
 
 
 def row_call(kernel, block, ins, weights, outs, sums, name, flops):
@@ -792,6 +754,256 @@
         cost_estimate=cost(flops, flops / 500),
         name=name,
     )(*ins, *[w[0] for w in weights])
+
+
+def write_masks(kind, target_row, source_row, row_ref, target_ref, source_ref):
+    places = lax.broadcasted_iota(jnp.int32, (LONG, 1), 0)
+    long = kind == 1
+    segment = jnp.where(long, 0, lax.shift_right_logical(places, 8))
+    offset = jnp.where(long, places, places & (SHORT - 1))
+    lane = lax.broadcasted_iota(jnp.int32, (1, WIDE), 1) & (HD - 1)
+    inside = segment == lane
+    row_ref[...] = jnp.where(inside | (lane == SEGS), 1.0, 0.0).astype(BF16)
+    ones = (lane > SEGS) & (lane < SEGS + 4)
+    for ref, lengths in ((target_ref, target_row), (source_ref, source_row)):
+        length = jnp.zeros((LONG, 1), jnp.int32)
+        for index in range(SEGS):
+            length = jnp.where(segment == index, lengths[index], length)
+        dead = offset >= length
+        blocked = ((lane < SEGS) & ~inside) | ((lane == SEGS) & dead)
+        ref[...] = jnp.where(blocked, NEG, jnp.where(ones, 1.0, 0.0)).astype(BF16)
+
+
+FORWARD_CHUNKS = 9
+FORWARD_LOCAL = 32
+
+
+def forward_kernel(*refs):
+    (
+        kind_ref, target_len, source_len,
+        self_b, cross_b, gain, shift, out_b, in_b,
+        tokens_hbm, encoded_hbm, self_in, self_out, cross_q, cross_kv, cross_out, ffn_in, ffn_out,
+        w_q_out, w_k_out, w_v_out, w_o_out, w_cq_out, w_ckv_out, w_co_full, w_fi_full, w_fo_full,
+        mixed_out, self_att_out, self_lse_out, resid_out, hidden_out, query_out, pairs_out,
+        cross_att_out, cross_lse_out, row_out, target_out, source_out, vec_ref, bias_ref,
+        w_q, w_k, w_v, w_o, w_cq, w_ckv,
+        tokens, encoded, mixed, self_att, self_lse, resid, hidden, query, pairs,
+        cross_att, cross_lse, row_side, target_side, source_side,
+        pack, pack16, small_full,
+        sems, small_sems, chunk_local, local,
+    ) = refs
+    used = [0]
+
+    def move(src, dst):
+        copy = pltpu.make_async_copy(src, dst, local.at[used[0]])
+        used[0] += 1
+        copy.start()
+        return copy
+
+    load_tokens, load_encoded = move(tokens_hbm, tokens), move(encoded_hbm, encoded)
+    rows = self_b.shape[1]
+    pack[...] = jnp.zeros_like(pack)
+    for start, ref in ((SELF_B, self_b), (CROSS_B, cross_b), (GAIN, gain), (SHIFT, shift), (OUT_B, out_b)):
+        pack[start : start + ref.shape[0], :rows] = ref[...].astype(F32)
+    pack[IN_B : IN_B + 1, : 4 * rows] = in_b[...].astype(F32)
+    pack16[...] = pack[...].astype(BF16)
+
+    greet()
+    chunks = [
+        (self_in.at[:, pl.ds(0, D)], w_q),
+        (self_in.at[:, pl.ds(D, D)], w_k),
+        (self_in.at[:, pl.ds(2 * D, D)], w_v),
+        (self_out, w_o),
+        (cross_q, w_cq),
+        (cross_kv, w_ckv),
+        (cross_out, w_co_full),
+        (ffn_in, w_fi_full),
+        (ffn_out, w_fo_full),
+    ]
+    plans = [
+        gather_steps(shard, full, sems.at[:, pl.ds(i * GATHER_COPIES, GATHER_COPIES)], chunk_local.at[i])
+        for i, (shard, full) in enumerate(chunks)
+    ]
+    small_plan = small_gather_steps(pack16, small_full, small_sems, chunk_local.at[FORWARD_CHUNKS])
+    first_group, second_group, third_group, fourth_group = (0, 1, 2), (3, 4, 5), (6, 7), (8,)
+
+    def step(group, number):
+        for index in group:
+            plans[index][number]()
+
+    small_plan[0]()
+    step(first_group, 0)
+    write_masks(
+        kind_ref[0],
+        [target_len[0, i] for i in range(SEGS)],
+        [source_len[0, i] for i in range(SEGS)],
+        row_side,
+        target_side,
+        source_side,
+    )
+    saves = [move(row_side, row_out), move(target_side, target_out), move(source_side, source_out)]
+    small_plan[1]()
+    step(first_group, 1)
+    step(second_group, 0)
+    small_plan[2]()
+    step(first_group, 2)
+    small_plan[3]()
+    for z in range(4):
+        for y in range(2):
+            for c in range(2):
+                owner = (z * 2 + y) * 2 + c
+                tile = small_full[z, y, c].astype(F32)
+                vec_ref[:, owner * rows : (owner + 1) * rows] = tile[:, :rows]
+                bias_ref[:, owner * 4 * rows : (owner + 1) * 4 * rows] = tile[IN_B : IN_B + 1, : 4 * rows]
+    step(first_group, 3)
+    step(second_group, 1)
+    step(third_group, 0)
+    step(first_group, 4)
+    saves += [move(w_q, w_q_out), move(w_k, w_k_out), move(w_v, w_v_out)]
+    load_tokens.wait()
+
+    def vec(row):
+        return vec_ref[row : row + 1, :]
+
+    def square(ref):
+        return ref[...].reshape(D, ref.shape[-1])
+
+    block = 512
+
+    @pl.loop(0, LONG // block)
+    def _(i):
+        part = pl.ds(pl.multiple_of(i * block, block), block)
+        left = tokens[part, :]
+        mixed[part, :D] = ((mm(left, square(w_q)) + vec(SELF_B)) * SCALE).astype(BF16)
+        mixed[part, D : 2 * D] = mm(left, square(w_k)).astype(BF16)
+        mixed[part, 2 * D :] = (mm(left, square(w_v)) + vec(SELF_B + 1)).astype(BF16)
+
+    saves.append(move(mixed, mixed_out))
+
+    def ticks(index, table):
+        for at, work in table.items():
+
+            @pl.when(index == at)
+            def _(work=work):
+                for group, number in work:
+                    step(group, number)
+
+    @pl.loop(0, PAIRS)
+    def _(pair):
+        def cols(offset):
+            return pl.ds(pl.multiple_of(offset + pair * WIDE, WIDE), WIDE)
+
+        attend(
+            True,
+            512,
+            mixed.at[:, cols(0)],
+            mixed.at[:, cols(D)],
+            mixed.at[:, cols(2 * D)],
+            row_side,
+            target_side,
+            self_att.at[:, cols(0)],
+            self_lse.at[pl.ds(pair, 1)],
+        )
+        ticks(
+            pair,
+            {
+                1: [(second_group, 2), (third_group, 1), (fourth_group, 0)],
+                3: [(second_group, 3)],
+            },
+        )
+
+    saves += [move(self_att, self_att_out), move(self_lse, self_lse_out)]
+    load_encoded.wait()
+    step(second_group, 4)
+    saves += [move(w_o, w_o_out), move(w_cq, w_cq_out), move(w_ckv, w_ckv_out)]
+
+    @pl.loop(0, LONG // block)
+    def _(i):
+        part = pl.ds(pl.multiple_of(i * block, block), block)
+        both = mm(encoded[part, :], square(w_ckv))
+        pairs[part, :D] = both[:, :D].astype(BF16)
+        pairs[part, D:] = (both[:, D:] + vec(CROSS_B + 1)).astype(BF16)
+        total = tokens[part, :].astype(F32) + mm(self_att[part, :], square(w_o)) + vec(SELF_B + 2)
+        resid[part, :] = total
+        xhat, _ = normed(total)
+        normal = (xhat * vec(GAIN) + vec(SHIFT)).astype(BF16)
+        hidden[part, :] = normal
+        query[part, :] = ((mm(normal, square(w_cq)) + vec(CROSS_B)) * SCALE).astype(BF16)
+
+    saves += [move(resid, resid_out), move(hidden, hidden_out), move(query, query_out), move(pairs, pairs_out)]
+    step(third_group, 2)
+    step(fourth_group, 1)
+
+    @pl.loop(0, PAIRS)
+    def _(pair):
+        def cols(offset):
+            return pl.ds(pl.multiple_of(offset + pair * WIDE, WIDE), WIDE)
+
+        attend(
+            False,
+            512,
+            query.at[:, cols(0)],
+            pairs.at[:, cols(0)],
+            pairs.at[:, cols(D)],
+            row_side,
+            source_side,
+            cross_att.at[:, cols(0)],
+            cross_lse.at[pl.ds(pair, 1)],
+        )
+        ticks(pair, {2: [(third_group, 3)], 4: [(fourth_group, 2)]})
+
+    saves += [move(cross_att, cross_att_out), move(cross_lse, cross_lse_out)]
+    step(fourth_group, 3)
+    step(third_group, 4)
+    step(fourth_group, 4)
+    for plan in plans + [small_plan]:
+        plan[-1]()
+    for copy in saves:
+        copy.wait()
+
+
+def forward_call(ints, smalls, arrays):
+    rows = smalls[0].shape[1]
+    square = gather_shape(rows, D)
+    lse = (PAIRS, LONG, 8)
+    wide = (LONG, WIDE)
+
+    def bf(*shape):
+        return jax.ShapeDtypeStruct(shape, BF16)
+
+    def f32(*shape):
+        return jax.ShapeDtypeStruct(shape, F32)
+
+    held = [bf(*square)] * 5 + [bf(*gather_shape(rows, 2 * D))]
+    saved = [
+        bf(LONG, 3 * D), bf(LONG, D), f32(*lse), f32(LONG, D), bf(LONG, D), bf(LONG, D), bf(LONG, 2 * D),
+        bf(LONG, D), f32(*lse), bf(*wide), bf(*wide), bf(*wide),
+    ]
+    outs = held + [bf(*square), bf(*gather_shape(rows, FF)), bf(*gather_shape(4 * rows, D))]
+    outs += saved + [f32(16, D), f32(1, FF)]
+    in_vmem = pl.BlockSpec(memory_space=pltpu.VMEM)
+    scratch = [pltpu.VMEM(s.shape, s.dtype) for s in held + [bf(LONG, D), bf(LONG, D)] + saved]
+    scratch += [
+        pltpu.VMEM((16, 256), F32),
+        pltpu.VMEM((16, 256), BF16),
+        pltpu.VMEM((4, 2, 2, 16, 256), BF16),
+        pltpu.SemaphoreType.DMA((2, FORWARD_CHUNKS * GATHER_COPIES)),
+        pltpu.SemaphoreType.DMA((2, SMALL_COPIES)),
+        pltpu.SemaphoreType.DMA((FORWARD_CHUNKS + 1,)),
+        pltpu.SemaphoreType.DMA((FORWARD_LOCAL,)),
+    ]
+    return pl.pallas_call(
+        forward_kernel,
+        out_shape=outs,
+        in_specs=[pl.BlockSpec(memory_space=pltpu.SMEM)] * len(ints)
+        + [in_vmem] * len(smalls)
+        + [any_spec()] * len(arrays),
+        out_specs=[any_spec()] * (len(outs) - 2) + [in_vmem] * 2,
+        scratch_shapes=scratch,
+        compiler_params=params(collective_id=0, has_side_effects=True),
+        cost_estimate=cost(14 * LONG * D * D + 8 * LONG * LONG * D, 60 << 20),
+        name="gather_forward",
+    )(*ints, *smalls, *arrays)
 
 
 def ffn_grads(activ_ref, branch3_ref, hidden2_ref, dpre_ref, out_grad_ref, in_grad_ref):
@@ -868,72 +1080,63 @@
     rows = self_in.shape[0]
     owners = D // rows
     direct = owners == 16
-    row_side, target_side, source_side = mask_lanes(bucket[0], target_len[0], source_len[0])
-
-    small = jnp.concatenate(
-        [
-            self_bias.reshape(-1),
-            cross_bias.reshape(-1),
-            norm_gain.reshape(-1),
-            norm_shift.reshape(-1),
-            ffn_out_bias,
-            ffn_in_bias,
-        ]
-    )
-    mixed_w = jnp.concatenate([self_out, cross_q, cross_kv, cross_out], axis=1)
+    square = (D, D)
     if direct:
-        small = jnp.pad(small, (0, PACK - small.shape[0])).reshape(16, 128)
-        self_w, small_all = gather_call([self_in], small, 0, "gather_self")
-        (mixed_w,) = gather_call([mixed_w], None, 1, "gather_cross")
-        ffn_in_w, ffn_out_w = gather_call([ffn_in, ffn_out], None, 2, "gather_ffn")
-        small_all = small_all.reshape(16, PACK)
+        smalls = [self_bias, cross_bias, norm_gain, norm_shift]
+        smalls += [ffn_out_bias.reshape(1, rows), ffn_in_bias.reshape(1, 4 * rows)]
+        arrays = [tokens, encoded, self_in, self_out, cross_q, cross_kv, cross_out, ffn_in, ffn_out]
+        results = forward_call([bucket, target_len, source_len], smalls, arrays)
+        weights = [w.reshape(16 * w.shape[3], w.shape[4]) for w in results[:9]]
+        (mixed, self_att, self_lse, resid1, hidden1, query, pairs, cross_att, cross_lse) = results[9:18]
+        row_side, target_side, source_side, vec, bias = results[18:]
     else:
         everyone = partial(lax.all_gather, axis_name="fsdp", axis=0, tiled=True)
-        self_w, mixed_w, ffn_in_w, ffn_out_w = map(everyone, (self_in, mixed_w, ffn_in, ffn_out))
-        small_all = lax.all_gather(small, "fsdp", axis=0, tiled=False)
-    self_w, mixed_w = self_w.reshape(D, 3 * D), mixed_w.reshape(D, 5 * D)
-    ffn_in_w, ffn_out_w = ffn_in_w.reshape(D, FF), ffn_out_w.reshape(FF, D)
-    small_all = small_all.astype(F32)
-    vec = small_all[:, : IN_B * rows].reshape(owners, IN_B, rows).transpose(1, 0, 2).reshape(IN_B, D)
-    vec = jnp.pad(vec, ((0, 3), (0, 0)))
-    bias = small_all[:, IN_B * rows : VEC_ROWS * rows].reshape(1, FF)
+        self_w = everyone(self_in)
+        weights = [self_w[:, i * D : (i + 1) * D] for i in range(3)]
+        weights += [everyone(w) for w in (self_out, cross_q, cross_kv, cross_out, ffn_in, ffn_out)]
+        small = [self_bias, cross_bias, norm_gain, norm_shift, ffn_out_bias, ffn_in_bias]
+        small_all = everyone(jnp.concatenate([w.reshape(1, -1) for w in small], axis=1)).astype(F32)
+        vec = small_all[:, : IN_B * rows].reshape(owners, IN_B, rows).transpose(1, 0, 2).reshape(IN_B, D)
+        vec = jnp.pad(vec, ((0, 3), (0, 0)))
+        bias = small_all[:, IN_B * rows : VEC_ROWS * rows].reshape(1, FF)
+        row_side, target_side, source_side = mask_lanes(bucket[0], target_len[0], source_len[0])
+        (mixed,) = row_call(
+            project_in,
+            512,
+            [tokens],
+            [(w, square, (0, 0)) for w in weights[:3]] + [(vec, (16, D), (0, 0))],
+            [(3 * D, BF16)],
+            [],
+            "project_in",
+            6 * LONG * D * D,
+        )
+        self_att, self_lse = attention_forward(
+            (mixed, 0), (mixed, PAIRS), (mixed, 2 * PAIRS), row_side, target_side, True, "self_forward"
+        )
+        resid1, hidden1, query, pairs = row_call(
+            between,
+            512,
+            [tokens, self_att, encoded],
+            [(weights[3], square, (0, 0)), (weights[4], square, (0, 0)), (weights[5], (D, 2 * D), (0, 0))]
+            + [(vec, (16, D), (0, 0))],
+            [(D, F32), (D, BF16), (D, BF16), (2 * D, BF16)],
+            [],
+            "between",
+            8 * LONG * D * D,
+        )
+        cross_att, cross_lse = attention_forward(
+            (query, 0), (pairs, 0), (pairs, PAIRS), row_side, source_side, False, "cross_forward"
+        )
+    w_q, w_k, w_v, w_o, w_cq, w_ckv, w_co, w_fi, w_fo = weights
     vec_weight = (vec, (16, D), (0, 0))
-    square = (D, D)
-
-    (mixed,) = row_call(
-        project_in,
-        512,
-        [tokens],
-        [(self_w, (D, 3 * D), (0, 0)), vec_weight],
-        [(3 * D, BF16)],
-        [],
-        "project_in",
-        6 * LONG * D * D,
-    )
-    self_att, self_lse = attention_forward(
-        (mixed, 0), (mixed, PAIRS), (mixed, 2 * PAIRS), row_side, target_side, True, "self_forward"
-    )
-    resid1, hidden1, query, pairs = row_call(
-        between,
-        512,
-        [tokens, self_att, encoded],
-        [(mixed_w, square, (0, 0)), (mixed_w, square, (0, 1)), (mixed_w, (D, 2 * D), (0, 1)), vec_weight],
-        [(D, F32), (D, BF16), (D, BF16), (2 * D, BF16)],
-        [],
-        "between",
-        8 * LONG * D * D,
-    )
-    cross_att, cross_lse = attention_forward(
-        (query, 0), (pairs, 0), (pairs, PAIRS), row_side, source_side, False, "cross_forward"
-    )
     (output, activ, branch3, dpre, hidden2, dresid2, branch2, d_cross_att, sums_mid, bias_sum) = row_call(
         middle,
         256,
         [hidden1, cross_att, cotangent],
         [
-            (mixed_w, square, (0, 4)),
-            (ffn_in_w, (D, FF), (0, 0)),
-            (ffn_out_w, (FF, D), (0, 0)),
+            (w_co, square, (0, 0)),
+            (w_fi, (D, FF), (0, 0)),
+            (w_fo, (FF, D), (0, 0)),
             vec_weight,
             (bias, (1, FF), (0, 0)),
         ],
@@ -959,7 +1162,7 @@
         after_cross,
         512,
         [dcq, dck, dcv, dresid2, resid1],
-        [(mixed_w, square, (0, 1)), (mixed_w, (D, 2 * D), (0, 1)), (mixed_w, square, (0, 0)), vec_weight],
+        [(w_cq, square, (0, 0)), (w_ckv, (D, 2 * D), (0, 0)), (w_o, square, (0, 0)), vec_weight],
         [(D, BF16), (D, F32), (D, BF16), (D, BF16)],
         [(8, D)],
         "after_cross",
@@ -987,7 +1190,7 @@
         tokens_back,
         512,
         [dq, dk, dv, dresid1],
-        [(self_w, (D, 3 * D), (0, 0))],
+        [(w, square, (0, 0)) for w in weights[:3]],
         [(D, BF16)],
         [],
         "tokens_back",

time: 587 us -> 469 us (0.80)
  Pallas kernels: 547 us -> 439 us
  local copies, waits for them, and re-layouts: 22.1 us -> 15.7 us
    pallas_call x5 -> x1, Pallas kernels: 182 us -> 98.9 us  [forward_call(): pl.pallas_call(forward_kernel, out_shape=outs, in_specs=[pl.BlockSpec(mem...]
    pallas_call x5 -> x3, Pallas kernels: 78.1 us -> 58.9 us  [row_call(): pl.pallas_call(kernel, grid=(LONG // block,), in_specs=in_specs, out_spec...]
where the time goes in v2:
time: 469 us; the launch traced here: 460 us
  Pallas kernels  439 us (94%)
  local copies, waits for them, and re-layouts  15.7 us (3%)
    pallas_call x3, Pallas kernels, scatter_call(): pl.pallas_call(partial(scatter_kernel, count, int(small is not None)), ou...  175 us
    pallas_call x1, Pallas kernels, forward_call(): pl.pallas_call(forward_kernel, out_shape=outs, in_specs=[pl.BlockSpec(mem...  98.9 us
    pallas_call x2, Pallas kernels, attention_backward(): pl.pallas_call(partial(attend_back, causal, 256 if causal else 512), grid...  67.2 us
    pallas_call x3, Pallas kernels, row_call(): pl.pallas_call(kernel, grid=(LONG // block,), in_specs=in_specs, out_spec...  58.9 us
    pallas_call x2, Pallas kernels, pair_grads_call(): pl.pallas_call(partial(pair_grads, count), grid=(count,), in_specs=[whole...  24.2 us
    pallas_call x1, Pallas kernels, ffn_grads_call(): pl.pallas_call(ffn_grads, grid=(FF // tile,), in_specs=[pl.BlockSpec((LON...  14.7 us

profile of v2, /device:TPU:0, one launch (start us, length us, event | category | flops | bytes accessed | tf_op | source)
XLA Modules:
  0.0 460.2 jit_solution(6837081304996733889)
XLA Ops:
  0.6 1.2 reshape.114.refs_8_
  2.5 98.9 %gather_forward.1 = (bf16[4,2,2,48,768]{4,3,2,1,0:T(8,128)(2,1)}, bf16[4,2,2,48,768]{4,3,2,1,0:T(8,128)(2,1)}, bf16[4,2,2,48,768]{4,3,2,1,0:T(8,128)(2,1)}, bf16...) custom-call(s32[1]{0:T(128)S(6)} %copy.47.refs_0_, ...), custom_call_target="tpu_custom_call" | custom-call | flops 14898167808 | bytes 62914560 | tf_op jit(solution)/shard_map/gather_forward/pallas_call | solution.py:995
  101.4 37.5 %middle.1 = (bf16[1024,768]{1,0:T(8,128)(2,1)}, bf16[1024,3072]{1,0:T(8,128)(2,1)}, bf16[1024,768]{1,0:T(8,128)(2,1)}, bf16[1024,3072]{1,0:T(8,128)(2,1)}, bf16[...) custom-call(bf16[1024,768]{1,0:T(8,128)(2,1)} %get-tuple-element.66., ...), custom_call_target="tpu_custom_call" | custom-call | flops 21743271936 | bytes 43486544 | tf_op jit(solution)/shard_map/middle/pallas_call | solution.py:747
  138.9 14.7 %ffn_grads.1 = (bf16[3072,768]{1,0:T(8,128)(2,1)}, bf16[768,3072]{1,0:T(8,128)(2,1)}) custom-call(bf16[1024,3072]{1,0:T(8,128)(2,1)} %get-tuple-element.108.activ_ref, bf16[1024,768]{1,0:T(8,128)(2,1)} %get-tuple-element.109.branch3_ref, bf16[1024,768]{1,0:T(8,128)(2,1)} %get-tuple-element.110.hidden2_ref, bf16[1024,3072]{1,0:T(8,128)(2,1)} %get-tuple-element.111.dpre_ref), custom_call_target="tpu_custom_call" | custom-call | flops 9663676416 | bytes 25165824 | tf_op jit(solution)/shard_map/ffn_grads/pallas_call | solution.py:1016
  153.6 76.1 %scatter_ffn.1 = (f32[48,3072]{1,0:T(8,128)}, f32[192,768]{1,0:T(8,128)}) custom-call(bf16[4,2,2,48,3072]{4,3,2,1,0:T(8,128)(2,1)} %bitcast.26, bf16[4,2,2,192,768]{4,3,2,1,0:T(8,128)(2,1)} %bitcast.25), custom_call_target="tpu_custom_call" | custom-call | tf_op jit(solution)/shard_map/scatter_ffn/pallas_call | solution.py:430
  229.7 39.1 %cross_backward.1 = (bf16[1024,768]{1,0:T(8,128)(2,1)}, bf16[1024,768]{1,0:T(8,128)(2,1)}, bf16[1024,768]{1,0:T(8,128)(2,1)}) custom-call(bf16[1024,768]{1,0:T(8,128)(2,1)} %get-tuple-element.76.q_ref, bf16[1024,1536]{1,0:T(8,128)(2,1)} %get-tuple-element.77.k_ref.v_ref, bf16[1024,1536]{1,0:T(8,128)(2,1)} %get-tuple-element.77.k_ref.v_ref, ...), custom_call_target="tpu_custom_call" | custom-call | flops 8053063680 | bytes 12582912 | tf_op jit(solution)/shard_map/cross_backward/pallas_call | solution.py:586
  268.8 13.0 %after_cross.1 = (bf16[1024,768]{1,0:T(8,128)(2,1)}, f32[1024,768]{1,0:T(8,128)}, bf16[1024,768]{1,0:T(8,128)(2,1)}, bf16[1024,768]{1,0:T(8,128)(2,1)}, f32[8,768]{1,0:T(8,128)}) custom-call(bf16[1024,768]{1,0:T(8,128)(2,1)} %get-tuple-element.82.dq_ref.refs_6_, bf16[1024,768]{1,0:T(8,128)(2,1)} %get-tuple-element.83.dk_ref.refs_7_, ...), custom_call_target="tpu_custom_call" | custom-call | flops 4831838208 | bytes 9663676 | tf_op jit(solution)/shard_map/after_cross/pallas_call | solution.py:747
  281.8 14.4 %cross_grads.1 = bf16[768,3840]{1,0:T(8,128)(2,1)} custom-call(bf16[1024,768]{1,0:T(8,128)(2,1)} %get-tuple-element.75.att_ref.refs_0_, bf16[1024,768]{1,0:T(8,128)(2,1)} %get-tuple-element.66.hidden1_ref.refs_1_, bf16[1024,768]{1,0:T(8,128)(2,1)} %refs_3_.3, bf16[1024,768]{1,0:T(8,128)(2,1)} %refs_3_.3, ...), custom_call_target="tpu_custom_call" | custom-call | flops 6039797760 | bytes 15728640 | tf_op jit(solution)/shard_map/cross_grads/pallas_call | solution.py:1047
  296.3 58.7 %scatter_cross.1 = f32[48,3840]{1,0:T(8,128)} custom-call(bf16[4,2,2,48,3840]{4,3,2,1,0:T(8,128)(2,1)} %bitcast.24), custom_call_target="tpu_custom_call" | custom-call | tf_op jit(solution)/shard_map/scatter_cross/pallas_call | solution.py:430
  355.0 1.8 fusion.1
  356.8 1.7 slice.61
  358.5 28.1 %self_backward.1 = (bf16[1024,768]{1,0:T(8,128)(2,1)}, bf16[1024,768]{1,0:T(8,128)(2,1)}, bf16[1024,768]{1,0:T(8,128)(2,1)}) custom-call(bf16[1024,2304]{1,0:T(8,128)(2,1)} %get-tuple-element.74.q_ref.k_ref.v_ref, bf16[1024,2304]{1,0:T(8,128)(2,1)} %get-tuple-element.74.q_ref.k_ref.v_ref, bf16[1024,2304]{1,0:T(8,128)(2,1)} %get-tuple-element.74.q_ref.k_ref.v_ref, ...), custom_call_target="tpu_custom_call" | custom-call | flops 8053063680 | bytes 12582912 | tf_op jit(solution)/shard_map/self_backward/pallas_call | solution.py:586
  386.6 0.0 copy-start.4
  386.6 0.0 copy-start.3
  386.6 0.0 copy-start.5
  386.6 2.4 convert_reduce_fusion
  389.0 0.1 concatenate.25
  389.1 0.1 concatenate.26
  389.2 0.0 copy-done.4
  389.2 0.1 concatenate.27
  389.3 0.1 concatenate.29
  389.4 0.1 concatenate.31
  389.5 0.0 copy-done.3
  389.5 0.1 concatenate.30
  389.6 0.1 concatenate.32
  389.7 0.1 concatenate.28
  389.8 0.1 concatenate.33
  389.9 0.3 concatenate.34
  390.1 0.1 reshape.125
  390.2 0.5 broadcast.15
  390.7 0.0 copy-done.5
  390.7 0.7 reduce.11
  391.4 0.1 reshape.126
  391.5 0.1 fusion
  391.6 0.7 copy.43
  392.3 9.8 %self_grads.1 = bf16[768,2304]{1,0:T(8,128)(2,1)} custom-call(bf16[1024,768]{1,0:T(8,128)(2,1)} %refs_2_.4, bf16[1024,768]{1,0:T(8,128)(2,1)} %refs_2_.4, bf16[1024,768]{1,0:T(8,128)(2,1)} %refs_2_.4, bf16[1024,768]{1,0:T(8,128)(2,1)} %get-tuple-element.93.dq_ref.refs_3_, bf16[1024,768]{1,0:T(8,128)(2,1)} %get-tuple-element.94.dk_ref.refs_4_, ...), custom_call_target="tpu_custom_call" | custom-call | flops 3623878656 | bytes 9437184 | tf_op jit(solution)/shard_map/self_grads/pallas_call | solution.py:1047
  402.0 40.7 %scatter_self.1 = (f32[48,2304]{1,0:T(8,128)}, f32[16,128]{1,0:T(8,128)}) custom-call(bf16[4,2,2,48,2304]{4,3,2,1,0:T(8,128)(2,1)} %bitcast.27, f32[4,2,2,16,128]{4,3,2,1,0:T(8,128)} %bitcast.28), custom_call_target="tpu_custom_call" | custom-call | tf_op jit(solution)/shard_map/scatter_self/pallas_call | solution.py:430
  442.7 0.9 fusion.3
  443.6 0.7 reshape.129
  444.3 0.7 reshape.131
  445.0 0.7 reshape.134
  445.6 0.7 reshape.135
  446.3 1.3 slice.70
  447.6 1.3 slice.71
  448.9 0.0 copy-start.2
  448.9 0.0 copy-start.1
  448.9 8.5 %tokens_back.1 = bf16[1024,768]{1,0:T(8,128)(2,1)} custom-call(bf16[1024,768]{1,0:T(8,128)(2,1)} %get-tuple-element.93.dq_ref.refs_3_, bf16[1024,768]{1,0:T(8,128)(2,1)} %get-tuple-element.94.dk_ref.refs_4_, bf16[1024,768]{1,0:T(8,128)(2,1)} %get-tuple-element.95.dv_ref.refs_5_, f32[1024,768]{1,0:T(8,128)} %get-tuple-element.96.dresid1_ref, ...), custom_call_target="tpu_custom_call" | custom-call | flops 3623878656 | bytes 7247757 | tf_op jit(solution)/shard_map/tokens_back/pallas_call | solution.py:747
  457.3 0.0 copy-start
  457.3 0.0 copy-done.2
  457.3 0.8 copy.48
  458.1 0.0 copy-done.1
  458.1 0.8 copy.49
  458.9 0.0 copy-done
  458.9 0.8 copy.50
  (7 shorter events, 0.1 us)
Async XLA Ops:
  386.6 2.6 copy-start.4
  386.6 2.9 copy-start.3
  386.6 4.1 copy-start.5
  448.9 8.5 %copy-start.2 = (f32[48,2304]{1,0:T(8,128)S(1)}, f32[48,2304]{1,0:T(8,128)}, u32[]{:S(2)}) copy-start(f32[48,2304]{1,0:T(8,128)} %get-tuple-element.150) | copy-start | bytes 1327108
  448.9 9.2 %copy-start.1 = (f32[48,3072]{1,0:T(8,128)S(1)}, f32[48,3072]{1,0:T(8,128)}, u32[]{:S(2)}) copy-start(f32[48,3072]{1,0:T(8,128)} %get-tuple-element.157) | copy-start | bytes 1769476
  457.3 1.6 copy-start
